TPU v7x, 256 devices: a whole 4x4x8 slice. The times are simulated.
256 devices in a mesh: depth: 32 (over x_hi, z, core), freq: 8 (over x_lo, y).
Axes of the slice: x: 4 (x_hi: 2, x_lo: 2; x = x_hi * 2 + x_lo), y: 4, z: 8, core: 2. Of those that a mesh axis runs over, the one named last changes fastest.
Arguments:
- propagator: bfloat16 [32, 16, 2, 1024, 1024], P('depth', 'freq'), may hold values from -0.125 to 0.125
- incident: bfloat16 [32, 16, 1024, 256], P('depth', 'freq'), may hold values from -6 to 6
- coeffs: float32 [32, 1024, 64], P('depth'), may hold values from -4 to 4
Outputs:
- upgoing: bfloat16 [32, 16, 1024, 256], P('depth', 'freq')
- gradient: float32 [32, 1024, 64], P('depth', 'freq')
- reflected: bfloat16 [32, 16, 1024, 256], P('depth', 'freq')
All inputs are finite; a program needn't handle non-finite values.
Results may differ from a plain program's by a relative error of at most 0.024.
Values may be sent and summed in bfloat16 or wider, within the bound.
No kernel may reach another device: no remote copies, remote signals or barrier semaphores. Data moves between devices by JAX's collectives and lax.ppermute only.
A program may use at most 64 MiB of HBM per device.

v0:
```python
import jax
import jax.numpy as jnp
from jax import lax
from jax.sharding import PartitionSpec as P

ITERS = 3


def passed_along(block, axis, distance):
    devices = range(lax.axis_size(axis))
    route = [(i - distance, i) for i in devices if i - distance in devices]
    return lax.ppermute(block, axis, route)


def angle_table(count, points):
    angle = jnp.arange(count, dtype=jnp.float32)[:, None] + 0.5
    place = jnp.arange(points, dtype=jnp.float32)[None, :] + 0.5
    return (jnp.sqrt(2.0 / points) * jnp.cos(jnp.pi * angle * place / points)).astype(jnp.bfloat16)


def angles_of(table, field):
    return jnp.einsum("ay,fys->fas", table, field, preferred_element_type=jnp.float32).astype(
        jnp.bfloat16
    )


def reflect(kernel, table, field):
    return jnp.einsum(
        "xa,fas->fxs", kernel, angles_of(table, field), preferred_element_type=jnp.float32
    )


def apply_level(weights, field, transpose):
    form = "fyx,fys->fxs" if transpose else "fxy,fys->fxs"
    first = jnp.einsum(form, weights[:, 0], field, preferred_element_type=jnp.float32)
    second = jnp.einsum(form, weights[:, 1], field, preferred_element_type=jnp.float32)
    half = field.shape[-1] // 2
    return first + jnp.concatenate([-second[..., half:], second[..., :half]], -1)


def local(propagator, incident, coeffs):
    weights = propagator[0]
    source = incident[0]
    count = coeffs.shape[2]
    points = incident.shape[2]
    width = incident.shape[3]
    nfreq = source.shape[0]
    table = angle_table(count, points)
    kernel = (coeffs[0] * table.T.astype(jnp.float32)).astype(jnp.bfloat16)
    down = jnp.zeros(source.shape, jnp.bfloat16)
    upgoing = jnp.zeros(source.shape, jnp.bfloat16)
    for step in range(ITERS):
        send_down = (down.astype(jnp.float32) - reflect(kernel, table, upgoing)).astype(
            jnp.bfloat16
        )
        total = (source.astype(jnp.float32) + down.astype(jnp.float32)).astype(jnp.bfloat16)
        send_up = (upgoing.astype(jnp.float32) + reflect(kernel, table, total)).astype(jnp.bfloat16)
        above = passed_along(send_down, "depth", 1)
        below = passed_along(send_up, "depth", -1)
        down = apply_level(weights, above, False).astype(jnp.bfloat16)
        upgoing = apply_level(weights, below, True).astype(jnp.bfloat16)
    total = (source.astype(jnp.float32) + down.astype(jnp.float32)).astype(jnp.bfloat16)
    final_angles = angles_of(table, total)
    scale = 1.0 / jnp.sqrt(jnp.float32(width // 2 * nfreq * lax.axis_size("freq")))
    partial_value = (
        jnp.einsum("fxs,fas->xa", upgoing, final_angles, preferred_element_type=jnp.float32) * scale
    )
    rows = points // lax.axis_size("freq")
    start = lax.axis_index("freq") * rows
    grad_rows = lax.psum_scatter(
        partial_value.astype(jnp.bfloat16), "freq", scatter_dimension=0, tiled=True
    ).astype(jnp.float32)
    mine = lax.dynamic_slice_in_dim(coeffs[0], start, rows, 0) - grad_rows
    updated = lax.all_gather(mine.astype(jnp.bfloat16), "freq", axis=0, tiled=True).astype(
        mine.dtype
    )
    new_kernel = (updated * table.T.astype(jnp.float32)).astype(jnp.bfloat16)
    reflected = jnp.einsum(
        "xa,fas->fxs", new_kernel, final_angles, preferred_element_type=jnp.float32
    ).astype(jnp.bfloat16)
    return (upgoing[None], grad_rows[None], reflected[None])


def solution(mesh):
    return jax.shard_map(
        local,
        mesh=mesh,
        in_specs=(
            P("depth", "freq", None, None, None),
            P("depth", "freq", None, None),
            P("depth", None, None),
        ),
        out_specs=(
            P("depth", "freq", None, None),
            P("depth", "freq", None),
            P("depth", "freq", None, None),
        ),
        check_vma=False,
    )
```

profile of v0, /device:TPU:6, one launch (start us, length us, event | category | flops | bytes accessed | tf_op | source)
XLA Modules:
  0.0 194.7 jit_solution(17160662192455812224)
XLA Ops:
  7.2 2.0 %fusion.63 = bf16[1024,64,1]{0,1,2:T(8,128)(2,1)S(1)} fusion(f32[1,1024,64]{1,2,0:T(8,128)} %param.5, f32[1024]{0:T(1024)S(1)} %iota_add_fusion, f32[64]{0:T(128)S(1)} %add_multiply_fusion), kind=kLoop, calls=%fused_computation.90 | loop fusion | flops 458752 | bytes 397568 | tf_op jit(solution)/shard_map/convert_element_type | solution.py:49
  9.2 2.5 %fusion.31 = bf16[2,1024,256]{1,2,0:T(8,128)(2,1)} fusion(bf16[1024,64,1]{0,1,2:T(8,128)(2,1)S(1)} %fusion.63, f32[1024]{0:T(1024)S(1)} %iota_add_fusion, f32[64]{0:T(128)S(1)} %add_multiply_fusion), kind=kOutput, calls=%fused_computation.50 | convolution fusion | flops 135561216 | bytes 1184000 | tf_op jit(solution)/shard_map/xa,fas->fxs/dot_general | solution.py:28
  11.7 1.9 collective-permute-start.1
  13.6 1.5 fusion.32
  15.1 8.1 %collective-permute-start = (bf16[2,1024,256]{1,2,0:T(8,128)(2,1)S(1)}, bf16[2,1024,256]{1,2,0:T(8,128)(2,1)S(1)}, u32[]{:S(2)}, u32[]{:S(2)}) collective-permute-start(bf16[2,1024,256]{1,2,0:T(8,128)(2,1)S(1)} %fusion.32), channel_id=1, source_target_pairs={{8,0},{16,8},{24,16},{32,24},{40,32},{48,40},{56,48},{64,56},{72,6... | collective-permute-start | bytes 3145736 | tf_op jit(solution)/shard_map/ppermute | solution.py:12
  23.2 7.6 %copy.23 = bf16[1,2,2,1024,1024]{4,3,1,2,0:T(8,128)(2,1)} copy(bf16[1,2,2,1024,1024]{4,3,2,1,0:T(8,128)(2,1)} %param.3) | data formatting | bytes 16777216 | tf_op args[0]
  30.8 1.6 collective-permute-done.1
  32.4 3.9 %fusion.26 = f32[2,1024,256]{1,2,0:T(8,128)S(1)} fusion(bf16[2,1024,256]{1,2,0:T(8,128)(2,1)S(1)} %collective-permute-done.1, bf16[2,2,1024,1024]{3,2,0,1:T(8,128)(2,1)} %bitcast.207), kind=kOutput, calls=%fused_computation.43 | convolution fusion | flops 1073741824 | bytes 7340032 | tf_op jit(solution)/shard_map/fxy,fys->fxs/dot_general | solution.py:36
  36.5 0.9 copy-done
  37.4 1.3 fusion.25
  38.8 0.2 slice_negate_fusion.5
  38.9 1.1 copy-done.5
  40.0 1.4 fusion.6
  41.4 1.3 fusion.5
  42.7 2.5 %fusion = bf16[2,1024,256]{1,2,0:T(8,128)(2,1)} fusion(bf16[2,1024,256]{1,2,0:T(8,128)(2,1)S(1)} %fusion.6, bf16[1024,64,1]{0,1,2:T(8,128)(2,1)S(1)} %fusion.63, bf16[2,1024,256]{1,2,0:T(8,128)(2,1)S(1)} %fusion.5, f32[1024]{0:T(1024)S(1)} %iota_add_fusion, f32[64]{0:T(128)S(1)} %add_multiply_fusion), kind=kOutput, calls=%fused_computation.8 | convolution fusion | flops 136085504 | bytes 3281152 | tf_op jit(solution)/shard_map/xa,fas->fxs/dot_general | solution.py:28
  45.2 2.1 %collective-permute-start.3 = (bf16[2,1024,256]{1,2,0:T(8,128)(2,1)}, bf16[2,1024,256]{1,2,0:T(8,128)(2,1)}, u32[]{:S(2)}, u32[]{:S(2)}) collective-permute-start(bf16[2,1024,256]{1,2,0:T(8,128)(2,1)} %fusion), channel_id=1, source_target_pairs={{0,8},{8,16},{16,24},{24,32},{32,40},{40,48},{48,56},{56,64},{64,7... | collective-permute-start | bytes 3145736 | tf_op jit(solution)/shard_map/ppermute | solution.py:12
  47.3 0.5 copy.12
  47.9 2.9 %fusion.12 = bf16[2,1024,256]{1,2,0:T(8,128)(2,1)S(1)} fusion(bf16[2,1024,256]{1,2,0:T(8,128)(2,1)} %copy-done.2, bf16[1024,64,1]{0,1,2:T(8,128)(2,1)S(1)} %fusion.63, bf16[2,1024,256]{1,2,0:T(8,128)(2,1)S(1)} %fusion.6, bf16[1,2,1024,256]{2,3,1,0:T(8,128)(2,1)S(1)} %copy.12, f32[1024]{0:T(1024)S(1)} %iota_add_fusion, f32[64]{0:T(128)S(1)} %add_multiply_fusion), kind=kOutput, calls=%fused_computation.28 | convolution fusion | flops 138182656 | bytes 4329728 | tf_op jit(solution)/shard_map/xa,fas->fxs/dot_general | solution.py:28
  50.8 7.3 %collective-permute-start.2 = (bf16[2,1024,256]{1,2,0:T(8,128)(2,1)S(1)}, bf16[2,1024,256]{1,2,0:T(8,128)(2,1)S(1)}, u32[]{:S(2)}, u32[]{:S(2)}) collective-permute-start(bf16[2,1024,256]{1,2,0:T(8,128)(2,1)S(1)} %fusion.12), channel_id=1, source_target_pairs={{8,0},{16,8},{24,16},{32,24},{40,32},{48,40},{56,48},{64,56},{72,6... | collective-permute-start | bytes 3145736 | tf_op jit(solution)/shard_map/ppermute | solution.py:12
  58.1 7.2 %collective-permute-done.3 = bf16[2,1024,256]{1,2,0:T(8,128)(2,1)} collective-permute-done((bf16[2,1024,256]{1,2,0:T(8,128)(2,1)}, bf16[2,1024,256]{1,2,0:T(8,128)(2,1)}, u32[]{:S(2)}, u32[]{:S(2)}) %collective-permute-start.3) | collective-permute-done | bytes 1048608 | tf_op jit(solution)/shard_map/ppermute | solution.py:12
  65.3 3.8 %fusion.28 = f32[2,1024,256]{1,2,0:T(8,128)S(1)} fusion(bf16[2,1024,256]{1,2,0:T(8,128)(2,1)} %collective-permute-done.3, bf16[2,2,1024,1024]{3,2,0,1:T(8,128)(2,1)} %bitcast.208), kind=kOutput, calls=%fused_computation.45 | convolution fusion | flops 1073741824 | bytes 7340032 | tf_op jit(solution)/shard_map/fxy,fys->fxs/dot_general | solution.py:36
  69.3 1.1 collective-permute-done.2
  70.4 4.1 %fusion.27 = f32[2,1024,256]{1,2,0:T(8,128)S(1)} fusion(bf16[2,1024,256]{1,2,0:T(8,128)(2,1)S(1)} %collective-permute-done.2, bf16[2,2,1024,1024]{3,2,0,1:T(8,128)(2,1)} %bitcast.209), kind=kOutput, calls=%fused_computation.44 | convolution fusion | flops 1073741824 | bytes 7340032 | tf_op jit(solution)/shard_map/fyx,fys->fxs/dot_general | solution.py:36
  74.5 0.2 slice_negate_fusion.3
  74.6 2.6 %fusion.8 = bf16[2,1024,256]{1,2,0:T(8,128)(2,1)S(1)} fusion(f32[2,1024,128]{1,2,0:T(8,128)S(1)} %get-tuple-element.14, f32[2,1024,128]{1,2,0:T(8,128)S(1)} %get-tuple-element.13, bf16[2,1024,256]{1,2,0:T(8,128)(2,1)} %collective-permute-done.3, bf16[2,2,1024,1024]{3,2,0,1:T(8,128)(2,1)S(1)} %bitcast.219), kind=kOutput, calls=%fused_computation.20 | convolution fusion | flops 1075314688 | bytes 8388608 | tf_op jit(solution)/shard_map/fxy,fys->fxs/dot_general | solution.py:35
  77.2 1.3 fusion.7
  78.5 2.5 %fusion.1 = bf16[2,1024,256]{1,2,0:T(8,128)(2,1)} fusion(bf16[2,1024,256]{1,2,0:T(8,128)(2,1)S(1)} %fusion.8, bf16[1024,64,1]{0,1,2:T(8,128)(2,1)S(1)} %fusion.63, bf16[2,1024,256]{1,2,0:T(8,128)(2,1)S(1)} %fusion.7, f32[1024]{0:T(1024)S(1)} %iota_add_fusion, f32[64]{0:T(128)S(1)} %add_multiply_fusion), kind=kOutput, calls=%fused_computation.9 | convolution fusion | flops 136085504 | bytes 3281152 | tf_op jit(solution)/shard_map/xa,fas->fxs/dot_general | solution.py:28
  81.1 1.9 collective-permute-start.5
  83.0 2.7 %fusion.11 = bf16[2,1024,256]{1,2,0:T(8,128)(2,1)} fusion(bf16[2,1024,256]{1,2,0:T(8,128)(2,1)S(1)} %fusion.7, bf16[1024,64,1]{0,1,2:T(8,128)(2,1)S(1)} %fusion.63, bf16[2,1024,256]{1,2,0:T(8,128)(2,1)S(1)} %fusion.8, bf16[1,2,1024,256]{2,3,1,0:T(8,128)(2,1)S(1)} %copy.12, f32[1024]{0:T(1024)S(1)} %iota_add_fusion, f32[64]{0:T(128)S(1)} %add_multiply_fusion), kind=kOutput, calls=%fused_computation.26 | convolution fusion | flops 138182656 | bytes 4329728 | tf_op jit(solution)/shard_map/xa,fas->fxs/dot_general | solution.py:28
  85.6 7.5 %collective-permute-start.4 = (bf16[2,1024,256]{1,2,0:T(8,128)(2,1)}, bf16[2,1024,256]{1,2,0:T(8,128)(2,1)S(1)}, u32[]{:S(2)}, u32[]{:S(2)}) collective-permute-start(bf16[2,1024,256]{1,2,0:T(8,128)(2,1)} %fusion.11), channel_id=1, source_target_pairs={{8,0},{16,8},{24,16},{32,24},{40,32},{48,40},{56,48},{64,56},{72,6... | collective-permute-start | bytes 3145736 | tf_op jit(solution)/shard_map/ppermute | solution.py:12
  93.1 8.0 %collective-permute-done.5 = bf16[2,1024,256]{1,2,0:T(8,128)(2,1)} collective-permute-done((bf16[2,1024,256]{1,2,0:T(8,128)(2,1)}, bf16[2,1024,256]{1,2,0:T(8,128)(2,1)}, u32[]{:S(2)}, u32[]{:S(2)}) %collective-permute-start.5) | collective-permute-done | bytes 1048608 | tf_op jit(solution)/shard_map/ppermute | solution.py:12
  101.1 3.8 %fusion.30 = f32[2,1024,256]{1,2,0:T(8,128)S(1)} fusion(bf16[2,1024,256]{1,2,0:T(8,128)(2,1)} %collective-permute-done.5, bf16[2,2,1024,1024]{3,2,0,1:T(8,128)(2,1)} %bitcast.210), kind=kOutput, calls=%fused_computation.47 | convolution fusion | flops 1073741824 | bytes 7340032 | tf_op jit(solution)/shard_map/fxy,fys->fxs/dot_general | solution.py:36
  104.9 0.3 slice_negate_fusion
  105.2 0.3 collective-permute-done.4
  105.5 3.8 %fusion.29 = f32[2,1024,256]{1,2,0:T(8,128)S(1)} fusion(bf16[2,1024,256]{1,2,0:T(8,128)(2,1)S(1)} %collective-permute-done.4, bf16[2,2,1024,1024]{3,2,0,1:T(8,128)(2,1)} %bitcast.211), kind=kOutput, calls=%fused_computation.46 | convolution fusion | flops 1073741824 | bytes 7340032 | tf_op jit(solution)/shard_map/fyx,fys->fxs/dot_general | solution.py:36
  109.3 1.5 slice_negate_fusion.1
  110.8 4.7 %fusion.38 = bf16[2,64,256]{2,1,0:T(8,128)(2,1)S(1)} fusion(f32[2,1024,128]{1,2,0:T(8,128)S(1)} %get-tuple-element.10, f32[2,1024,128]{1,2,0:T(8,128)S(1)} %get-tuple-element.9, bf16[2,1024,256]{1,2,0:T(8,128)(2,1)} %collective-permute-done.5, bf16[2,2,1024,1024]{3,2,0,1:T(8,128)(2,1)} %bitcast.212, bf16[1,2,1024,256]{2,3,1,0:T(8,128)(2,1)S(1)} %copy.12, ...), kind=kOutput, calls=%fused_computation.64 | convolution fusion | flops 1144815616 | bytes 8458496 | tf_op jit(solution)/shard_map/ay,fys->fas/dot_general | solution.py:22
  115.5 4.4 %fusion.9 = bf16[2,1024,256]{1,2,0:T(8,128)(2,1)S(1)} fusion(f32[2,1024,128]{1,2,0:T(8,128)} %get-tuple-element.12, f32[2,1024,128]{1,2,0:T(8,128)} %get-tuple-element.11, bf16[2,1024,256]{1,2,0:T(8,128)(2,1)} %copy-done.3, bf16[2,2,1024,1024]{3,2,0,1:T(8,128)(2,1)} %bitcast.213), kind=kOutput, calls=%fused_computation.22 | convolution fusion | flops 1075314688 | bytes 8388608 | tf_op jit(solution)/shard_map/fyx,fys->fxs/dot_general | solution.py:35
  119.9 0.3 fusion.36
  120.2 0.8 copy.20
  121.1 1.3 copy.16
  122.4 36.8 %reduce-scatter.4.cloned.1.call-done = bf16[128,64]{1,0:T(8,128)(2,1)} async-done(((bf16[1024,64]{1,0:T(8,128)(2,1)}), bf16[128,64]{1,0:T(8,128)(2,1)}) %reduce-scatter.4.cloned.1.call-update) | async-done | bytes 16400
  159.1 0.8 copy.21
  160.0 0.6 convert_bitcast_fusion
  160.6 0.8 fusion.120
  161.4 23.8 %all_gather.3 = bf16[1024,64]{0,1:T(8,128)(2,1)S(1)} all-gather(bf16[128,64]{0,1:T(8,128)(2,1)S(1)} %fusion.120), channel_id=1, replica_groups=mesh['depth'=32,'freq'=8] {'freq'}, dimensions={0}, use_global_device_ids=true | all-gather | bytes 147456 | tf_op jit(solution)/shard_map/all_gather | solution.py:74
  185.2 1.3 fusion.33
  186.5 1.3 copy.17
  (22 shorter events, 0.4 us)
Async XLA Ops:
  7.2 6.4 %copy-start.1 = (bf16[1,2,1024,256]{3,2,1,0:T(8,128)(2,1)S(1)}, bf16[1,2,1024,256]{3,2,1,0:T(8,128)(2,1)}, u32[]{:S(2)}) copy-start(bf16[1,2,1024,256]{3,2,1,0:T(8,128)(2,1)} %param.4) | copy-start | bytes 3145732
  7.2 152.0 %reduce-scatter.4.cloned.1.call-start = ((), (), s32[]{:S(2)}) async-start(), calls=%async_computation.1 | async-start | bytes 294912
  11.7 20.7 %collective-permute-start.1 = (bf16[2,1024,256]{1,2,0:T(8,128)(2,1)}, bf16[2,1024,256]{1,2,0:T(8,128)(2,1)S(1)}, u32[]{:S(2)}, u32[]{:S(2)}) collective-permute-start(bf16[2,1024,256]{1,2,0:T(8,128)(2,1)} %fusion.31), channel_id=1, source_target_pairs={{0,8},{8,16},{16,24},{24,32},{32,40},{40,48},{48,56},{56,64},{64,7... | collective-permute-start | bytes 3145736 | tf_op jit(solution)/shard_map/ppermute | solution.py:12
  15.1 21.4 %collective-permute-start = (bf16[2,1024,256]{1,2,0:T(8,128)(2,1)S(1)}, bf16[2,1024,256]{1,2,0:T(8,128)(2,1)S(1)}, u32[]{:S(2)}, u32[]{:S(2)}) collective-permute-start(bf16[2,1024,256]{1,2,0:T(8,128)(2,1)S(1)} %fusion.32), channel_id=1, source_target_pairs={{8,0},{16,8},{24,16},{32,24},{40,32},{48,40},{56,48},{64,56},{72,6... | collective-permute-start | bytes 3145736 | tf_op jit(solution)/shard_map/ppermute | solution.py:12
  32.4 3.9 %copy-start.4 = (bf16[2,1024,256]{1,2,0:T(8,128)(2,1)}, bf16[2,1024,256]{1,2,0:T(8,128)(2,1)S(1)}, u32[]{:S(2)}) copy-start(bf16[2,1024,256]{1,2,0:T(8,128)(2,1)S(1)} %collective-permute-done.1) | copy-start | bytes 3145732
  32.4 5.0 %copy-start = (bf16[1,2,2,1024,1024]{4,3,1,2,0:T(8,128)(2,1)S(1)}, bf16[1,2,2,1024,1024]{4,3,1,2,0:T(8,128)(2,1)}, u32[]{:S(2)}) copy-start(bf16[1,2,2,1024,1024]{4,3,1,2,0:T(8,128)(2,1)} %copy.23) | copy-start | bytes 25165828
  38.7 1.2 copy-start.5
  42.7 2.5 %copy-start.2 = (bf16[2,1024,256]{1,2,0:T(8,128)(2,1)}, bf16[2,1024,256]{1,2,0:T(8,128)(2,1)S(1)}, u32[]{:S(2)}) copy-start(bf16[2,1024,256]{1,2,0:T(8,128)(2,1)S(1)} %fusion.5) | copy-start | bytes 3145732
  45.2 20.0 %collective-permute-start.3 = (bf16[2,1024,256]{1,2,0:T(8,128)(2,1)}, bf16[2,1024,256]{1,2,0:T(8,128)(2,1)}, u32[]{:S(2)}, u32[]{:S(2)}) collective-permute-start(bf16[2,1024,256]{1,2,0:T(8,128)(2,1)} %fusion), channel_id=1, source_target_pairs={{0,8},{8,16},{16,24},{24,32},{32,40},{40,48},{48,56},{56,64},{64,7... | collective-permute-start | bytes 3145736 | tf_op jit(solution)/shard_map/ppermute | solution.py:12
  50.8 19.6 %collective-permute-start.2 = (bf16[2,1024,256]{1,2,0:T(8,128)(2,1)S(1)}, bf16[2,1024,256]{1,2,0:T(8,128)(2,1)S(1)}, u32[]{:S(2)}, u32[]{:S(2)}) collective-permute-start(bf16[2,1024,256]{1,2,0:T(8,128)(2,1)S(1)} %fusion.12), channel_id=1, source_target_pairs={{8,0},{16,8},{24,16},{32,24},{40,32},{48,40},{56,48},{64,56},{72,6... | collective-permute-start | bytes 3145736 | tf_op jit(solution)/shard_map/ppermute | solution.py:12
  69.1 5.5 %slice-start = ((s8[8388608]{0:T(1024)(128)(4,1)}), s8[4194304]{0:T(1024)(128)(4,1)S(1)}, s32[]{:S(2)}) async-start(s8[8388608]{0:T(1024)(128)(4,1)} %bitcast.217), calls=%async_computation.2 | async-start | bytes 8388608
  69.3 5.4 %slice-start.1 = ((s8[8388608]{0:T(1024)(128)(4,1)}), s8[4194304]{0:T(1024)(128)(4,1)S(1)}, s32[]{:S(2)}) async-start(s8[8388608]{0:T(1024)(128)(4,1)} %bitcast.217), calls=%async_computation.3 | async-start | bytes 8388608
  81.1 20.0 %collective-permute-start.5 = (bf16[2,1024,256]{1,2,0:T(8,128)(2,1)}, bf16[2,1024,256]{1,2,0:T(8,128)(2,1)}, u32[]{:S(2)}, u32[]{:S(2)}) collective-permute-start(bf16[2,1024,256]{1,2,0:T(8,128)(2,1)} %fusion.1), channel_id=1, source_target_pairs={{0,8},{8,16},{16,24},{24,32},{32,40},{40,48},{48,56},{56,64},{64,7... | collective-permute-start | bytes 3145736 | tf_op jit(solution)/shard_map/ppermute | solution.py:12
  85.6 19.9 %collective-permute-start.4 = (bf16[2,1024,256]{1,2,0:T(8,128)(2,1)}, bf16[2,1024,256]{1,2,0:T(8,128)(2,1)S(1)}, u32[]{:S(2)}, u32[]{:S(2)}) collective-permute-start(bf16[2,1024,256]{1,2,0:T(8,128)(2,1)} %fusion.11), channel_id=1, source_target_pairs={{8,0},{16,8},{24,16},{32,24},{40,32},{48,40},{56,48},{64,56},{72,6... | collective-permute-start | bytes 3145736 | tf_op jit(solution)/shard_map/ppermute | solution.py:12
  105.5 3.8 %copy-start.3 = (bf16[2,1024,256]{1,2,0:T(8,128)(2,1)}, bf16[2,1024,256]{1,2,0:T(8,128)(2,1)S(1)}, u32[]{:S(2)}) copy-start(bf16[2,1024,256]{1,2,0:T(8,128)(2,1)S(1)} %collective-permute-done.4) | copy-start | bytes 3145732
Sparse Core Ops, SparseCore 0:
  121.2 37.8 reduce-scatter.3
where the time goes:
time: 196 us; the launch traced here: 195 us
  waiting for transfers between devices  55 us (28%)
  matrix products  52.6 us (27%)
  starting transfers between devices  28.7 us (15%)
  blocking collectives  23.8 us (12%)
  local copies, waits for them, and re-layouts  14.5 us (7%)
  between operations  14.4 us (7%)
  other arithmetic  5.72 us (3%)
    unnamed x2, waiting for transfers between devices  36.8 us
    ppermute x6, starting transfers between devices, passed_along(): return lax.ppermute(block, axis, route)  28.7 us
    all_gather x1, blocking collectives, local(): lax.all_gather(mine.astype(jnp.bfloat16), 'freq', axis=0, tiled=True)  23.8 us
    dot_general x6, matrix products, apply_level(): jnp.einsum(form, weights[:, 1], field, preferred_element_type=jnp.float32)  20.7 us
    ppermute x6, waiting for transfers between devices, passed_along(): return lax.ppermute(block, axis, route)  18.3 us
    dot_general x6, matrix products, reflect(): jnp.einsum('xa,fas->fxs', kernel, angles_of(table, field), preferred_elem...  14.6 us
    unnamed x22, local copies, waits for them, and re-layouts  14.5 us
    dot_general x5, matrix products, apply_level(): jnp.einsum(form, weights[:, 0], field, preferred_element_type=jnp.float32)  11 us
  transfers between devices with their start and end apart: 7, of which 6 were waited for; matrix products, arithmetic and copies ran while one was open for 15% of the time, Pallas kernels for 0%

commit v1 on v0

v1 whole, which is shorter than its diff:
```python
import jax
import jax.numpy as jnp
from jax import lax
from jax.sharding import PartitionSpec as P

BF = jnp.bfloat16
F32 = jnp.float32


def passed_along(block, axis, distance):
    devices = range(lax.axis_size(axis))
    route = [(i - distance, i) for i in devices if i - distance in devices]
    return lax.ppermute(block, axis, route)


def angle_table(count, points):
    angle = jnp.arange(count, dtype=F32)[:, None] + 0.5
    place = jnp.arange(points, dtype=F32)[None, :] + 0.5
    return (jnp.sqrt(2.0 / points) * jnp.cos(jnp.pi * angle * place / points)).astype(BF)


def dot(form, a, b):
    return jnp.einsum(form, a, b, preferred_element_type=F32)


def turned(field):
    half = field.shape[-1] // 2
    return jnp.concatenate([-field[..., half:], field[..., :half]], -1)


def both(field):
    return jnp.concatenate([field, turned(field)], -2)


def times(pair, field):
    return dot("fab,fbs->fas", pair, both(field))


def joined(panel):
    nfreq, _, count, points = panel.shape
    return panel.reshape(nfreq, 2 * count, points)


def advance(weights, panel):
    real, imag = panel[:, 0], panel[:, 1]
    left = jnp.concatenate(
        [jnp.concatenate([real, -imag], -1), jnp.concatenate([imag, real], -1)], 1
    )
    nfreq, _, rows, points = weights.shape
    out = dot("fax,fxy->fay", left, weights.reshape(nfreq, 2 * rows, points)).astype(BF)
    return out.reshape(nfreq, 2, -1, points)


def summed(value, axis):
    size = lax.axis_size(axis)
    step = size // 2
    while step:
        small = value.astype(BF)
        other = lax.ppermute(small, axis, [(i, i ^ step) for i in range(size)])
        value = small.astype(F32) + other.astype(F32)
        step //= 2
    return value


def local(propagator, incident, coeffs):
    weights = propagator[0]
    source = incident[0]
    count = coeffs.shape[2]
    points = incident.shape[2]
    width = incident.shape[3]
    nfreq = source.shape[0]
    table = angle_table(count, points)
    kernel = (coeffs[0].T * table.astype(F32)).astype(BF)

    def up(x):
        return passed_along(x, "depth", -1)

    def down(x):
        return passed_along(x, "depth", 1)

    start = dot("ax,fxs->fas", table, source).astype(BF)
    kernel_below = up(kernel)
    start1 = up(start)
    kernel_above = down(kernel)
    seen = dot("ax,fcxy->fcay", table, weights).astype(BF)
    m = dot("ax,fcxy->fcay", kernel_below, weights).astype(BF)
    m_below = up(m)
    start2 = up(start1)
    j = dot("fcxy,ay->fxca", weights, kernel_above).astype(BF).reshape(nfreq, points, 2 * count)
    j_above = down(j)
    g = dot("fcax,bx->facb", seen, kernel_above).astype(BF).reshape(nfreq, count, 2 * count)
    g_below = up(g)
    tm = dot("ax,fbx->fab", table, joined(m)).astype(BF)
    tu1 = times(tm, start1).astype(BF)
    tu1_above = down(tu1)
    n = advance(weights, m_below)
    n_below = up(n)
    start3 = up(start2)
    tn = dot("ax,fbx->fab", table, joined(n)).astype(BF)
    tu2 = (times(tn, start2) + times(tm, start1)).astype(BF)
    tu2_above = down(tu2)
    tu1_above2 = down(tu1_above)
    part_r = dot("fax,fxb->fab", seen[:, 0], j_above)
    part_i = dot("fax,fxb->fab", seen[:, 1], j_above)
    h = (part_r + turned(part_i)).astype(BF)
    td3 = times(h, tu1_above2) + times(g, tu2_above)
    final_angles = (start.astype(F32) - td3).astype(BF)
    b1 = (start1.astype(F32) - times(g_below, tu1)).astype(BF)
    q = advance(weights, n_below)
    panels = jnp.concatenate([joined(q), joined(n), joined(m)], 1)
    fields = jnp.concatenate([both(start3), both(start2), both(b1)], 1)
    upgoing = dot("fbx,fbs->fxs", panels, fields).astype(BF)

    scale = 1.0 / jnp.sqrt(jnp.float32(width // 2 * nfreq * lax.axis_size("freq")))
    gradient = summed(dot("fas,fxs->ax", final_angles, upgoing) * scale, "freq")
    rows = points // lax.axis_size("freq")
    grad_rows = lax.dynamic_slice_in_dim(gradient, lax.axis_index("freq") * rows, rows, 1).T
    new_kernel = ((coeffs[0].T - gradient) * table.astype(F32)).astype(BF)
    reflected = dot("ax,fas->fxs", new_kernel, final_angles).astype(BF)
    return (upgoing[None], grad_rows[None], reflected[None])


def solution(mesh):
    return jax.shard_map(
        local,
        mesh=mesh,
        in_specs=(
            P("depth", "freq", None, None, None),
            P("depth", "freq", None, None),
            P("depth", None, None),
        ),
        out_specs=(
            P("depth", "freq", None, None),
            P("depth", "freq", None),
            P("depth", "freq", None, None),
        ),
        check_vma=False,
    )
```

time: 196 us -> 124 us (0.63)
  waiting for transfers between devices: 55 us -> 25.4 us
  blocking collectives: 23.8 us -> 0 us
  starting transfers between devices: 28.7 us -> 52.5 us
  matrix products: 52.6 us -> 34.6 us
  between operations: 14.4 us -> 1.12 us
  local copies, waits for them, and re-layouts: 14.5 us -> 3.8 us
    unnamed x2 -> x0, waiting for transfers between devices: 36.8 us -> none
    all_gather x1 -> x0, blocking collectives: 23.8 us -> none  [local(): lax.all_gather(mine.astype(jnp.bfloat16), 'freq', axis=0, tiled=True)]
    ppermute x6 -> x12, starting transfers between devices: 28.7 us -> 47.5 us  [passed_along(): return lax.ppermute(block, axis, route)]
    dot_general x20 -> x16, matrix products: 52.6 us -> 34.6 us  [dot(): return jnp.einsum(form, a, b, preferred_element_type=F32)]
    unnamed x22 -> x23, local copies, waits for them, and re-layouts: 14.5 us -> 1.38 us
    ppermute x0 -> x3, waiting for transfers between devices: none -> 11.7 us  [summed(): other = lax.ppermute(small, axis, [(i, i ^ step) for i in range(size)])]
    ppermute x0 -> x3, starting transfers between devices: none -> 5.02 us  [summed(): other = lax.ppermute(small, axis, [(i, i ^ step) for i in range(size)])]
    ppermute x6 -> x12, waiting for transfers between devices: 18.3 us -> 13.7 us  [passed_along(): return lax.ppermute(block, axis, route)]
  transfers between devices with their start and end apart: 7 -> 15, of which waited for: 6 -> 6; matrix products, arithmetic and copies ran while one was open for 15% -> 25% of each run, Pallas kernels for 0% -> 0%
where the time goes in v1:
time: 124 us; the launch traced here: 123 us
  starting transfers between devices  52.5 us (42%)
  matrix products  34.6 us (28%)
  waiting for transfers between devices  25.4 us (20%)
  other arithmetic  5.79 us (5%)
  local copies, waits for them, and re-layouts  3.8 us (3%)
    ppermute x12, starting transfers between devices, passed_along(): return lax.ppermute(block, axis, route)  47.5 us
    dot_general x16, matrix products, dot(): return jnp.einsum(form, a, b, preferred_element_type=F32)  34.6 us
    ppermute x12, waiting for transfers between devices, passed_along(): return lax.ppermute(block, axis, route)  13.7 us
    ppermute x3, waiting for transfers between devices, summed(): other = lax.ppermute(small, axis, [(i, i ^ step) for i in range(size)])  11.7 us
    ppermute x3, starting transfers between devices, summed(): other = lax.ppermute(small, axis, [(i, i ^ step) for i in range(size)])  5.02 us
    neg x8, other arithmetic, turned(): return jnp.concatenate([-field[..., half:], field[..., :half]], -1)  2.73 us
  transfers between devices with their start and end apart: 15, of which 6 were waited for; matrix products, arithmetic and copies ran while one was open for 25% of the time, Pallas kernels for 0%

profile of v1, /device:TPU:6, one launch (start us, length us, event | category | flops | bytes accessed | tf_op | source)
XLA Modules:
  0.0 123.2 jit_solution(11947697319033319555)
XLA Ops:
  0.6 0.0 copy-start
  0.7 2.0 %fusion.51 = bf16[64,1024]{1,0:T(8,128)(2,1)S(1)} fusion(f32[1,1024,64]{1,2,0:T(8,128)} %param.5, f32[1024]{0:T(1024)S(1)} %iota_add_fusion, f32[64]{0:T(128)S(1)} %add_multiply_fusion), kind=kLoop, calls=%fused_computation.54 | loop fusion | flops 458752 | bytes 397568 | tf_op jit(solution)/shard_map/convert_element_type | solution.py:73
  2.6 8.0 %collective-permute-start = (bf16[64,1024]{1,0:T(8,128)(2,1)S(1)}, bf16[64,1024]{1,0:T(8,128)(2,1)S(1)}, u32[]{:S(2)}, u32[]{:S(2)}) collective-permute-start(bf16[64,1024]{1,0:T(8,128)(2,1)S(1)} %fusion.51), channel_id=1, source_target_pairs={{8,0},{16,8},{24,16},{32,24},{40,32},{48,40},{56,48},{64,56},{72,6... | collective-permute-start | bytes 393224 | tf_op jit(solution)/shard_map/ppermute | solution.py:13
  10.7 1.9 %collective-permute-start.6 = (bf16[64,1024]{1,0:T(8,128)(2,1)S(1)}, bf16[64,1024]{1,0:T(8,128)(2,1)S(1)}, u32[]{:S(2)}, u32[]{:S(2)}) collective-permute-start(bf16[64,1024]{1,0:T(8,128)(2,1)S(1)} %fusion.51), channel_id=1, source_target_pairs={{0,8},{8,16},{16,24},{24,32},{32,40},{40,48},{48,56},{56,64},{64,7... | collective-permute-start | bytes 393224 | tf_op jit(solution)/shard_map/ppermute | solution.py:13
  12.6 1.1 fusion.33
  13.7 7.5 %collective-permute-start.3 = (bf16[2,64,256]{2,1,0:T(8,128)(2,1)S(1)}, bf16[2,64,256]{2,1,0:T(8,128)(2,1)S(1)}, u32[]{:S(2)}, u32[]{:S(2)}) collective-permute-start(bf16[2,64,256]{2,1,0:T(8,128)(2,1)S(1)} %fusion.33), channel_id=1, source_target_pairs={{8,0},{16,8},{24,16},{32,24},{40,32},{48,40},{56,48},{64,56},{72,6... | collective-permute-start | bytes 196616 | tf_op jit(solution)/shard_map/ppermute | solution.py:13
  21.2 5.8 %fusion.25 = bf16[2,2,64,1024]{3,2,1,0:T(8,128)(2,1)S(1)} fusion(bf16[1,2,2,1024,1024]{4,3,2,1,0:T(8,128)(2,1)} %param.3, f32[1024]{0:T(1024)S(1)} %iota_add_fusion, f32[64]{0:T(128)S(1)} %add_multiply_fusion), kind=kOutput, calls=%fused_computation.20 | convolution fusion | flops 537395200 | bytes 8917248 | tf_op jit(solution)/shard_map/ax,fcxy->fcay/dot_general | solution.py:23
  27.1 3.3 %collective-permute-start.4 = (bf16[2,64,256]{2,1,0:T(8,128)(2,1)S(1)}, bf16[2,64,256]{2,1,0:T(8,128)(2,1)S(1)}, u32[]{:S(2)}, u32[]{:S(2)}) collective-permute-start(bf16[2,64,256]{2,1,0:T(8,128)(2,1)S(1)} %collective-permute-done.3), channel_id=1, source_target_pairs={{8,0},{16,8},{24,16},{32,24},{40,32},{48,40},{56,48},{64,56},{72,6... | collective-permute-start | bytes 196616 | tf_op jit(solution)/shard_map/ppermute | solution.py:13
  30.5 1.6 %fusion.16 = bf16[64,2,2,1024]{3,0,2,1:T(8,128)(2,1)S(1)} fusion(bf16[1,2,2,1024,1024]{4,3,2,1,0:T(8,128)(2,1)S(1)} %copy-done.1, bf16[64,1024]{1,0:T(8,128)(2,1)S(1)} %collective-permute-done), kind=kOutput, calls=%fused_computation.15 | convolution fusion | flops 537133056 | bytes 9043968 | tf_op jit(solution)/shard_map/ax,fcxy->fcay/dot_general | solution.py:23
  32.0 1.9 %collective-permute-start.1 = (bf16[2,2,64,1024]{3,2,1,0:T(8,128)(2,1)S(1)}, bf16[2,2,64,1024]{3,2,1,0:T(8,128)(2,1)S(1)}, u32[]{:S(2)}, u32[]{:S(2)}) collective-permute-start(bf16[2,2,64,1024]{3,2,1,0:T(8,128)(2,1)S(1)} %bitcast.129), channel_id=1, source_target_pairs={{8,0},{16,8},{24,16},{32,24},{40,32},{48,40},{56,48},{64,56},{72,6... | collective-permute-start | bytes 1572872 | tf_op jit(solution)/shard_map/ppermute | solution.py:13
  34.0 1.9 %fusion.147 = (bf16[2,64,256]{2,1,0:T(8,128)(2,1)}, f32[2,64,256]{2,1,0:T(8,128)}) fusion(bf16[2,64,128]{2,1,0:T(8,128)(2,1)S(1)} %get-tuple-element.21, bf16[2,64,128]{2,1,0:T(8,128)(2,1)S(1)} %get-tuple-element.20, bf16[2,64,256]{2,1,0:T(8,128)(2,1)S(1)} %collective-permute-done.3, bf16[2,128,1024]{2,1,0:T(8,128)(2,1)S(1)} %bitcast.130, ...), kind=kOutput, calls=%fused_computation.160 | convolution fusion | flops 42647552 | bytes 856320 | tf_op jit(solution)/shard_map/fab,fbs->fas/dot_general | solution.py:23
  35.9 2.4 %collective-permute-start.9 = (bf16[2,64,256]{2,1,0:T(8,128)(2,1)}, bf16[2,64,256]{2,1,0:T(8,128)(2,1)}, u32[]{:S(2)}, u32[]{:S(2)}) collective-permute-start(bf16[2,64,256]{2,1,0:T(8,128)(2,1)} %get-tuple-element.26), channel_id=1, source_target_pairs={{0,8},{8,16},{16,24},{24,32},{32,40},{40,48},{48,56},{56,64},{64,7... | collective-permute-start | bytes 196616 | tf_op jit(solution)/shard_map/ppermute | solution.py:13
  38.3 1.4 %slice_negate_fusion.4 = (bf16[2,64,128]{2,1,0:T(8,128)(2,1)}, bf16[2,64,128]{2,1,0:T(8,128)(2,1)}) fusion(bf16[2,64,256]{2,1,0:T(8,128)(2,1)} %get-tuple-element.26), kind=kLoop, calls=%fused_computation.129 | loop fusion | flops 16384 | bytes 131072 | tf_op jit(solution)/shard_map/neg | solution.py:28
  39.7 6.0 %fusion.22 = bf16[64,2,2,1024]{3,0,2,1:T(8,128)(2,1)S(1)} fusion(bf16[1,2,2,1024,1024]{4,3,2,1,0:T(8,128)(2,1)} %param.3, bf16[64,1024]{1,0:T(8,128)(2,1)S(1)} %collective-permute-done.6), kind=kOutput, calls=%fused_computation.17 | convolution fusion | flops 537133056 | bytes 9043968 | tf_op jit(solution)/shard_map/fcxy,ay->fxca/dot_general | solution.py:23
  45.7 1.0 copy.10
  46.7 2.3 %collective-permute-start.8 = (bf16[2,1024,128]{2,1,0:T(8,128)(2,1)}, bf16[2,1024,128]{2,1,0:T(8,128)(2,1)S(1)}, u32[]{:S(2)}, u32[]{:S(2)}) collective-permute-start(bf16[2,1024,128]{2,1,0:T(8,128)(2,1)} %copy.10), channel_id=1, source_target_pairs={{0,8},{8,16},{16,24},{24,32},{32,40},{40,48},{48,56},{56,64},{64,7... | collective-permute-start | bytes 1572872 | tf_op jit(solution)/shard_map/ppermute | solution.py:13
  49.0 0.4 convolution_convert_fusion.4
  49.4 0.7 copy.8
  50.1 6.9 %collective-permute-start.7 = (bf16[2,64,128]{2,1,0:T(8,128)(2,1)}, bf16[2,64,128]{2,1,0:T(8,128)(2,1)S(1)}, u32[]{:S(2)}, u32[]{:S(2)}) collective-permute-start(bf16[2,64,128]{2,1,0:T(8,128)(2,1)} %copy.8), channel_id=1, source_target_pairs={{8,0},{16,8},{24,16},{32,24},{40,32},{48,40},{56,48},{64,56},{72,6... | collective-permute-start | bytes 98312 | tf_op jit(solution)/shard_map/ppermute | solution.py:13
  57.0 2.0 %collective-permute-start.5 = (bf16[2,64,256]{2,1,0:T(8,128)(2,1)S(1)}, bf16[2,64,256]{2,1,0:T(8,128)(2,1)S(1)}, u32[]{:S(2)}, u32[]{:S(2)}) collective-permute-start(bf16[2,64,256]{2,1,0:T(8,128)(2,1)S(1)} %collective-permute-done.4), channel_id=1, source_target_pairs={{8,0},{16,8},{24,16},{32,24},{40,32},{48,40},{56,48},{64,56},{72,6... | collective-permute-start | bytes 196616 | tf_op jit(solution)/shard_map/ppermute | solution.py:13
  59.0 1.9 %collective-permute-done.5 = bf16[2,64,256]{2,1,0:T(8,128)(2,1)S(1)} collective-permute-done((bf16[2,64,256]{2,1,0:T(8,128)(2,1)S(1)}, bf16[2,64,256]{2,1,0:T(8,128)(2,1)S(1)}, u32[]{:S(2)}, u32[]{:S(2)}) %collective-permute-start.5) | collective-permute-done | bytes 65568 | tf_op jit(solution)/shard_map/ppermute | solution.py:13
  60.9 2.1 %collective-permute-start.10 = (bf16[2,64,256]{2,1,0:T(8,128)(2,1)}, bf16[2,64,256]{2,1,0:T(8,128)(2,1)S(1)}, u32[]{:S(2)}, u32[]{:S(2)}) collective-permute-start(bf16[2,64,256]{2,1,0:T(8,128)(2,1)} %collective-permute-done.9), channel_id=1, source_target_pairs={{0,8},{8,16},{16,24},{24,32},{32,40},{40,48},{48,56},{56,64},{64,7... | collective-permute-start | bytes 196616 | tf_op jit(solution)/shard_map/ppermute | solution.py:13
  63.0 1.1 constant_dynamic-update-slice_fusion
  64.2 6.2 %collective-permute-done.10 = bf16[2,64,256]{2,1,0:T(8,128)(2,1)S(1)} collective-permute-done((bf16[2,64,256]{2,1,0:T(8,128)(2,1)}, bf16[2,64,256]{2,1,0:T(8,128)(2,1)S(1)}, u32[]{:S(2)}, u32[]{:S(2)}) %collective-permute-start.10) | collective-permute-done | bytes 65568 | tf_op jit(solution)/shard_map/ppermute | solution.py:13
  70.4 0.6 slice_negate_fusion.2
  71.1 4.6 %convolution_convert_fusion.2 = bf16[2,128,1024]{2,1,0:T(8,128)(2,1)S(1)} fusion(bf16[2,2048,1024]{2,1,0:T(8,128)(2,1)} %bitcast.123, bf16[2,64,1024]{2,1,0:T(8,128)(2,1)S(1)} %get-tuple-element.9, bf16[2,64,1024]{2,1,0:T(8,128)(2,1)S(1)} %get-tuple-element.8, bf16[2,64,1024]{2,1,0:T(8,128)(2,1)S(1)} %fusion.145), kind=kOutput, calls=%fused_computation.19 | convolution fusion | flops 1078198272 | bytes 9699328 | tf_op jit(solution)/shard_map/fax,fxy->fay/dot_general | solution.py:23
  75.7 0.0 copy-start.8
  75.7 2.2 %fusion.32 = bf16[2,64,256]{2,1,0:T(8,128)(2,1)S(1)} fusion(f32[2,64,256]{2,1,0:T(8,128)} %get-tuple-element.27, bf16[2,128,1024]{2,1,0:T(8,128)(2,1)S(1)} %convolution_convert_fusion.2, bf16[2,64,128]{2,1,0:T(8,128)(2,1)S(1)} %get-tuple-element.23, bf16[2,64,128]{2,1,0:T(8,128)(2,1)S(1)} %get-tuple-element.22, ...), kind=kOutput, calls=%fused_computation.30 | convolution fusion | flops 42680320 | bytes 856320 | tf_op jit(solution)/shard_map/fab,fbs->fas/dot_general | solution.py:23
  78.0 1.9 %collective-permute-start.11 = (bf16[2,64,256]{2,1,0:T(8,128)(2,1)S(1)}, bf16[2,64,256]{2,1,0:T(8,128)(2,1)S(1)}, u32[]{:S(2)}, u32[]{:S(2)}) collective-permute-start(bf16[2,64,256]{2,1,0:T(8,128)(2,1)S(1)} %fusion.32), channel_id=1, source_target_pairs={{0,8},{8,16},{16,24},{24,32},{32,40},{40,48},{48,56},{56,64},{64,7... | collective-permute-start | bytes 196616 | tf_op jit(solution)/shard_map/ppermute | solution.py:13
  79.9 0.2 fusion.53
  80.2 0.6 slice_negate_fusion
  80.8 7.2 %collective-permute-start.2 = (bf16[2,2,64,1024]{3,2,1,0:T(8,128)(2,1)}, bf16[2,2,64,1024]{3,2,1,0:T(8,128)(2,1)S(1)}, u32[]{:S(2)}, u32[]{:S(2)}) collective-permute-start(bf16[2,2,64,1024]{3,2,1,0:T(8,128)(2,1)} %bitcast.132), channel_id=1, source_target_pairs={{8,0},{16,8},{24,16},{32,24},{40,32},{48,40},{56,48},{64,56},{72,6... | collective-permute-start | bytes 1572872 | tf_op jit(solution)/shard_map/ppermute | solution.py:13
  88.1 0.2 fusion.80
  88.3 1.2 fusion.31
  89.5 5.6 %collective-permute-done.2 = bf16[2,2,64,1024]{3,2,1,0:T(8,128)(2,1)S(1)} collective-permute-done((bf16[2,2,64,1024]{3,2,1,0:T(8,128)(2,1)}, bf16[2,2,64,1024]{3,2,1,0:T(8,128)(2,1)S(1)}, u32[]{:S(2)}, u32[]{:S(2)}) %collective-permute-start.2) | collective-permute-done | bytes 524320 | tf_op jit(solution)/shard_map/ppermute | solution.py:13
  95.1 4.7 %convolution_convert_fusion.1 = bf16[2,128,1024]{2,1,0:T(8,128)(2,1)S(1)} fusion(bf16[2,2048,1024]{2,1,0:T(8,128)(2,1)} %bitcast.124, bf16[2,64,1024]{2,1,0:T(8,128)(2,1)S(1)} %get-tuple-element.7, bf16[2,64,1024]{2,1,0:T(8,128)(2,1)S(1)} %get-tuple-element.6, bf16[2,64,1024]{2,1,0:T(8,128)(2,1)S(1)} %fusion.146), kind=kOutput, calls=%fused_computation.18 | convolution fusion | flops 1078198272 | bytes 9699328 | tf_op jit(solution)/shard_map/fax,fxy->fay/dot_general | solution.py:23
  99.9 0.8 fusion.12
  100.7 0.4 fusion.29
  101.2 0.1 collective-permute-start.12
  101.3 5.0 %collective-permute-done.12 = bf16[64,1024]{1,0:T(8,128)(2,1)S(1)} collective-permute-done((bf16[64,1024]{1,0:T(8,128)(2,1)S(1)}, bf16[64,1024]{1,0:T(8,128)(2,1)S(1)}, u32[]{:S(2)}, u32[]{:S(2)}) %collective-permute-start.12) | collective-permute-done | bytes 131104 | tf_op jit(solution)/shard_map/ppermute | solution.py:59
  106.3 3.3 %collective-permute-start.13 = (bf16[64,1024]{1,0:T(8,128)(2,1)S(1)}, bf16[64,1024]{1,0:T(8,128)(2,1)S(1)}, u32[]{:S(2)}, u32[]{:S(2)}) collective-permute-start(bf16[64,1024]{1,0:T(8,128)(2,1)S(1)} %add_convert_fusion.1), channel_id=1, source_target_pairs={{0,2},{1,3},{2,0},{3,1},{4,6},{5,7},{6,4},{7,5},{8,10},{9,11},{10,... | collective-permute-start | bytes 393224 | tf_op jit(solution)/shard_map/ppermute | solution.py:59
  109.6 3.3 %collective-permute-done.13 = bf16[64,1024]{1,0:T(8,128)(2,1)S(1)} collective-permute-done((bf16[64,1024]{1,0:T(8,128)(2,1)S(1)}, bf16[64,1024]{1,0:T(8,128)(2,1)S(1)}, u32[]{:S(2)}, u32[]{:S(2)}) %collective-permute-start.13) | collective-permute-done | bytes 131104 | tf_op jit(solution)/shard_map/ppermute | solution.py:59
  112.9 1.7 %collective-permute-start.14 = (bf16[64,1024]{1,0:T(8,128)(2,1)S(1)}, bf16[64,1024]{1,0:T(8,128)(2,1)}, u32[]{:S(2)}, u32[]{:S(2)}) collective-permute-start(bf16[64,1024]{1,0:T(8,128)(2,1)S(1)} %add_convert_fusion), channel_id=1, source_target_pairs={{0,1},{1,0},{2,3},{3,2},{4,5},{5,4},{6,7},{7,6},{8,9},{9,8},{10,11... | collective-permute-start | bytes 393224 | tf_op jit(solution)/shard_map/ppermute | solution.py:59
  114.5 3.5 %collective-permute-done.14 = bf16[64,1024]{1,0:T(8,128)(2,1)} collective-permute-done((bf16[64,1024]{1,0:T(8,128)(2,1)S(1)}, bf16[64,1024]{1,0:T(8,128)(2,1)}, u32[]{:S(2)}, u32[]{:S(2)}) %collective-permute-start.14) | collective-permute-done | bytes 131104 | tf_op jit(solution)/shard_map/ppermute | solution.py:59
  118.0 2.3 %fusion.15 = bf16[1,2,1024,256]{2,3,1,0:T(8,128)(2,1)S(1)} fusion(bf16[2,64,256]{2,1,0:T(8,128)(2,1)} %copy-done.4, f32[1,1024,64]{1,2,0:T(8,128)S(1)} %copy-done.3, f32[1024]{0:T(1024)S(1)} %iota_add_fusion, f32[64]{0:T(128)S(1)} %add_multiply_fusion, bf16[64,1024]{1,0:T(8,128)(2,1)} %collective-permute-done.14, bf16[64,1024]{1,0:T(8,128)(2,1)S(1)} %add_convert_fusion), kind=kOutput, calls=%fused_computation.14 | convolution fusion | flops 68354048 | bytes 1642752 | tf_op jit(solution)/shard_map/ax,fas->fxs/dot_general | solution.py:23
  120.3 1.3 %copy.12 = bf16[1,2,1024,256]{3,2,1,0:T(8,128)(2,1)} copy(bf16[1,2,1024,256]{2,3,1,0:T(8,128)(2,1)S(1)} %fusion.15) | data formatting | bytes 2097152
  121.6 0.9 convert_add_fusion
  122.6 0.6 dynamic-slice_bitcast_fusion
  (45 shorter events, 0.4 us)
Async XLA Ops:
  0.6 12.0 %copy-start = (bf16[1,2,1024,256]{3,2,1,0:T(8,128)(2,1)S(1)}, bf16[1,2,1024,256]{3,2,1,0:T(8,128)(2,1)}, u32[]{:S(2)}) copy-start(bf16[1,2,1024,256]{3,2,1,0:T(8,128)(2,1)} %param.4) | copy-start | bytes 3145732
  2.6 27.8 %collective-permute-start = (bf16[64,1024]{1,0:T(8,128)(2,1)S(1)}, bf16[64,1024]{1,0:T(8,128)(2,1)S(1)}, u32[]{:S(2)}, u32[]{:S(2)}) collective-permute-start(bf16[64,1024]{1,0:T(8,128)(2,1)S(1)} %fusion.51), channel_id=1, source_target_pairs={{8,0},{16,8},{24,16},{32,24},{40,32},{48,40},{56,48},{64,56},{72,6... | collective-permute-start | bytes 393224 | tf_op jit(solution)/shard_map/ppermute | solution.py:13
  10.7 29.0 %collective-permute-start.6 = (bf16[64,1024]{1,0:T(8,128)(2,1)S(1)}, bf16[64,1024]{1,0:T(8,128)(2,1)S(1)}, u32[]{:S(2)}, u32[]{:S(2)}) collective-permute-start(bf16[64,1024]{1,0:T(8,128)(2,1)S(1)} %fusion.51), channel_id=1, source_target_pairs={{0,8},{8,16},{16,24},{24,32},{32,40},{40,48},{48,56},{56,64},{64,7... | collective-permute-start | bytes 393224 | tf_op jit(solution)/shard_map/ppermute | solution.py:13
  13.7 16.8 %copy-start.1 = (bf16[1,2,2,1024,1024]{4,3,2,1,0:T(8,128)(2,1)S(1)}, bf16[1,2,2,1024,1024]{4,3,2,1,0:T(8,128)(2,1)}, u32[]{:S(2)}) copy-start(bf16[1,2,2,1024,1024]{4,3,2,1,0:T(8,128)(2,1)} %param.3) | copy-start | bytes 25165828
  13.7 13.4 %collective-permute-start.3 = (bf16[2,64,256]{2,1,0:T(8,128)(2,1)S(1)}, bf16[2,64,256]{2,1,0:T(8,128)(2,1)S(1)}, u32[]{:S(2)}, u32[]{:S(2)}) collective-permute-start(bf16[2,64,256]{2,1,0:T(8,128)(2,1)S(1)} %fusion.33), channel_id=1, source_target_pairs={{8,0},{16,8},{24,16},{32,24},{40,32},{48,40},{56,48},{64,56},{72,6... | collective-permute-start | bytes 196616 | tf_op jit(solution)/shard_map/ppermute | solution.py:13
  27.1 6.9 %copy-start.5 = (bf16[2,64,256]{2,1,0:T(8,128)(2,1)}, bf16[2,64,256]{2,1,0:T(8,128)(2,1)S(1)}, u32[]{:S(2)}) copy-start(bf16[2,64,256]{2,1,0:T(8,128)(2,1)S(1)} %collective-permute-done.3) | copy-start | bytes 196612
  27.1 29.9 %collective-permute-start.4 = (bf16[2,64,256]{2,1,0:T(8,128)(2,1)S(1)}, bf16[2,64,256]{2,1,0:T(8,128)(2,1)S(1)}, u32[]{:S(2)}, u32[]{:S(2)}) collective-permute-start(bf16[2,64,256]{2,1,0:T(8,128)(2,1)S(1)} %collective-permute-done.3), channel_id=1, source_target_pairs={{8,0},{16,8},{24,16},{32,24},{40,32},{48,40},{56,48},{64,56},{72,6... | collective-permute-start | bytes 196616 | tf_op jit(solution)/shard_map/ppermute | solution.py:13
  32.0 39.0 %collective-permute-start.1 = (bf16[2,2,64,1024]{3,2,1,0:T(8,128)(2,1)S(1)}, bf16[2,2,64,1024]{3,2,1,0:T(8,128)(2,1)S(1)}, u32[]{:S(2)}, u32[]{:S(2)}) collective-permute-start(bf16[2,2,64,1024]{3,2,1,0:T(8,128)(2,1)S(1)} %bitcast.129), channel_id=1, source_target_pairs={{8,0},{16,8},{24,16},{32,24},{40,32},{48,40},{56,48},{64,56},{72,6... | collective-permute-start | bytes 1572872 | tf_op jit(solution)/shard_map/ppermute | solution.py:13
  35.9 25.1 %collective-permute-start.9 = (bf16[2,64,256]{2,1,0:T(8,128)(2,1)}, bf16[2,64,256]{2,1,0:T(8,128)(2,1)}, u32[]{:S(2)}, u32[]{:S(2)}) collective-permute-start(bf16[2,64,256]{2,1,0:T(8,128)(2,1)} %get-tuple-element.26), channel_id=1, source_target_pairs={{0,8},{8,16},{16,24},{24,32},{32,40},{40,48},{48,56},{56,64},{64,7... | collective-permute-start | bytes 196616 | tf_op jit(solution)/shard_map/ppermute | solution.py:13
  46.7 33.2 %collective-permute-start.8 = (bf16[2,1024,128]{2,1,0:T(8,128)(2,1)}, bf16[2,1024,128]{2,1,0:T(8,128)(2,1)S(1)}, u32[]{:S(2)}, u32[]{:S(2)}) collective-permute-start(bf16[2,1024,128]{2,1,0:T(8,128)(2,1)} %copy.10), channel_id=1, source_target_pairs={{0,8},{8,16},{16,24},{24,32},{32,40},{40,48},{48,56},{56,64},{64,7... | collective-permute-start | bytes 1572872 | tf_op jit(solution)/shard_map/ppermute | solution.py:13
  50.1 13.0 %collective-permute-start.7 = (bf16[2,64,128]{2,1,0:T(8,128)(2,1)}, bf16[2,64,128]{2,1,0:T(8,128)(2,1)S(1)}, u32[]{:S(2)}, u32[]{:S(2)}) collective-permute-start(bf16[2,64,128]{2,1,0:T(8,128)(2,1)} %copy.8), channel_id=1, source_target_pairs={{8,0},{16,8},{24,16},{32,24},{40,32},{48,40},{56,48},{64,56},{72,6... | collective-permute-start | bytes 98312 | tf_op jit(solution)/shard_map/ppermute | solution.py:13
  57.0 3.8 %collective-permute-start.5 = (bf16[2,64,256]{2,1,0:T(8,128)(2,1)S(1)}, bf16[2,64,256]{2,1,0:T(8,128)(2,1)S(1)}, u32[]{:S(2)}, u32[]{:S(2)}) collective-permute-start(bf16[2,64,256]{2,1,0:T(8,128)(2,1)S(1)} %collective-permute-done.4), channel_id=1, source_target_pairs={{8,0},{16,8},{24,16},{32,24},{40,32},{48,40},{56,48},{64,56},{72,6... | collective-permute-start | bytes 196616 | tf_op jit(solution)/shard_map/ppermute | solution.py:13
  60.9 9.5 %collective-permute-start.10 = (bf16[2,64,256]{2,1,0:T(8,128)(2,1)}, bf16[2,64,256]{2,1,0:T(8,128)(2,1)S(1)}, u32[]{:S(2)}, u32[]{:S(2)}) collective-permute-start(bf16[2,64,256]{2,1,0:T(8,128)(2,1)} %collective-permute-done.9), channel_id=1, source_target_pairs={{0,8},{8,16},{16,24},{24,32},{32,40},{40,48},{48,56},{56,64},{64,7... | collective-permute-start | bytes 196616 | tf_op jit(solution)/shard_map/ppermute | solution.py:13
  64.1 6.9 %copy-start.6 = (bf16[2,384,256]{2,1,0:T(8,128)(2,1)}, bf16[2,384,256]{2,1,0:T(8,128)(2,1)S(1)}, u32[]{:S(2)}) copy-start(bf16[2,384,256]{2,1,0:T(8,128)(2,1)S(1)} %maximum_dynamic-update-slice_fusion) | copy-start | bytes 1179652
  75.7 4.2 %copy-start.8 = (bf16[2,128,1024]{2,1,0:T(8,128)(2,1)}, bf16[2,128,1024]{2,1,0:T(8,128)(2,1)S(1)}, u32[]{:S(2)}) copy-start(bf16[2,128,1024]{2,1,0:T(8,128)(2,1)S(1)} %convolution_convert_fusion.2) | copy-start | bytes 1572868
  78.0 10.1 %collective-permute-start.11 = (bf16[2,64,256]{2,1,0:T(8,128)(2,1)S(1)}, bf16[2,64,256]{2,1,0:T(8,128)(2,1)S(1)}, u32[]{:S(2)}, u32[]{:S(2)}) collective-permute-start(bf16[2,64,256]{2,1,0:T(8,128)(2,1)S(1)} %fusion.32), channel_id=1, source_target_pairs={{0,8},{8,16},{16,24},{24,32},{32,40},{40,48},{48,56},{56,64},{64,7... | collective-permute-start | bytes 196616 | tf_op jit(solution)/shard_map/ppermute | solution.py:13
  80.8 14.2 %collective-permute-start.2 = (bf16[2,2,64,1024]{3,2,1,0:T(8,128)(2,1)}, bf16[2,2,64,1024]{3,2,1,0:T(8,128)(2,1)S(1)}, u32[]{:S(2)}, u32[]{:S(2)}) collective-permute-start(bf16[2,2,64,1024]{3,2,1,0:T(8,128)(2,1)} %bitcast.132), channel_id=1, source_target_pairs={{8,0},{16,8},{24,16},{32,24},{40,32},{48,40},{56,48},{64,56},{72,6... | collective-permute-start | bytes 1572872 | tf_op jit(solution)/shard_map/ppermute | solution.py:13
  89.5 11.2 %copy-start.4 = (bf16[2,64,256]{2,1,0:T(8,128)(2,1)}, bf16[2,64,256]{2,1,0:T(8,128)(2,1)S(1)}, u32[]{:S(2)}) copy-start(bf16[2,64,256]{2,1,0:T(8,128)(2,1)S(1)} %fusion.31) | copy-start | bytes 196612
  95.1 4.8 %copy-start.7 = (bf16[2,384,256]{2,1,0:T(8,128)(2,1)S(1)}, bf16[2,384,256]{2,1,0:T(8,128)(2,1)}, u32[]{:S(2)}) copy-start(bf16[2,384,256]{2,1,0:T(8,128)(2,1)} %copy-done.6) | copy-start | bytes 1179652
  95.1 4.8 %copy-start.9 = (bf16[2,128,1024]{2,1,0:T(8,128)(2,1)S(1)}, bf16[2,128,1024]{2,1,0:T(8,128)(2,1)}, u32[]{:S(2)}) copy-start(bf16[2,128,1024]{2,1,0:T(8,128)(2,1)} %copy-done.8) | copy-start | bytes 1572868
  99.9 18.2 %copy-start.3 = (f32[1,1024,64]{1,2,0:T(8,128)S(1)}, f32[1,1024,64]{1,2,0:T(8,128)}, u32[]{:S(2)}) copy-start(f32[1,1024,64]{1,2,0:T(8,128)} %param.5) | copy-start | bytes 786436
  100.7 21.8 %copy-start.2 = (bf16[2,1024,256]{2,1,0:T(8,128)(2,1)}, bf16[2,1024,256]{2,1,0:T(8,128)(2,1)S(1)}, u32[]{:S(2)}) copy-start(bf16[2,1024,256]{2,1,0:T(8,128)(2,1)S(1)} %fusion.12) | copy-start | bytes 3145732
  101.2 5.1 %collective-permute-start.12 = (bf16[64,1024]{1,0:T(8,128)(2,1)S(1)}, bf16[64,1024]{1,0:T(8,128)(2,1)S(1)}, u32[]{:S(2)}, u32[]{:S(2)}) collective-permute-start(bf16[64,1024]{1,0:T(8,128)(2,1)S(1)} %fusion.29), channel_id=1, source_target_pairs={{0,4},{1,5},{2,6},{3,7},{4,0},{5,1},{6,2},{7,3},{8,12},{9,13},{10,... | collective-permute-start | bytes 393224 | tf_op jit(solution)/shard_map/ppermute | solution.py:59
  106.3 6.6 %collective-permute-start.13 = (bf16[64,1024]{1,0:T(8,128)(2,1)S(1)}, bf16[64,1024]{1,0:T(8,128)(2,1)S(1)}, u32[]{:S(2)}, u32[]{:S(2)}) collective-permute-start(bf16[64,1024]{1,0:T(8,128)(2,1)S(1)} %add_convert_fusion.1), channel_id=1, source_target_pairs={{0,2},{1,3},{2,0},{3,1},{4,6},{5,7},{6,4},{7,5},{8,10},{9,11},{10,... | collective-permute-start | bytes 393224 | tf_op jit(solution)/shard_map/ppermute | solution.py:59
  112.9 5.2 %collective-permute-start.14 = (bf16[64,1024]{1,0:T(8,128)(2,1)S(1)}, bf16[64,1024]{1,0:T(8,128)(2,1)}, u32[]{:S(2)}, u32[]{:S(2)}) collective-permute-start(bf16[64,1024]{1,0:T(8,128)(2,1)S(1)} %add_convert_fusion), channel_id=1, source_target_pairs={{0,1},{1,0},{2,3},{3,2},{4,5},{5,4},{6,7},{7,6},{8,9},{9,8},{10,11... | collective-permute-start | bytes 393224 | tf_op jit(solution)/shard_map/ppermute | solution.py:59

commit v2 on v0

v2 whole, which is shorter than its diff:
```python
import jax
import jax.numpy as jnp
import numpy as np
from jax import lax
from jax.experimental import pallas as pl
from jax.experimental.pallas import tpu as pltpu
from jax.sharding import PartitionSpec as P

BF = jnp.bfloat16
F32 = jnp.float32
MIB = 2**20


def exchanged(block, axis, first):
    size = lax.axis_size(axis)
    route = []
    for i in range(first, size - 1, 2):
        route += [(i, i + 1), (i + 1, i)]
    return lax.ppermute(block, axis, route)


def is_even(axis):
    return lax.rem(lax.axis_index(axis), 2) == 0


def angle_table(count, points):
    angle = np.arange(count, dtype=np.float32)[:, None] + np.float32(0.5)
    place = np.arange(points, dtype=np.float32)[None, :] + np.float32(0.5)
    wave = np.cos(np.float32(np.pi) * angle * place / np.float32(points))
    return jnp.asarray((np.sqrt(np.float32(2.0 / points)) * wave).astype(BF))


def dot(a, b):
    return jnp.dot(a, b, preferred_element_type=F32)


def dot_t(a, b):
    return lax.dot_general(a, b, (((1,), (1,)), ((), ())), preferred_element_type=F32)


def t_dot(a, b):
    return lax.dot_general(a, b, (((0,), (0,)), ((), ())), preferred_element_type=F32)


def turned(field):
    half = field.shape[-1] // 2
    return jnp.concatenate([-field[:, half:], field[:, :half]], -1)


def both(field):
    return jnp.concatenate([field, turned(field)], 0)


def pack(ref, row, col, value):
    width = value.shape[1]
    fold = min((ref.shape[1] - col) // width, value.shape[0] // 16)
    rows = value.shape[0] // fold
    for i in range(fold):
        ref[row : row + rows, col + i * width : col + (i + 1) * width] = value[
            i * rows : (i + 1) * rows
        ]


def unpack(ref, row, col, count, width):
    fold = min((ref.shape[1] - col) // width, count // 16)
    rows = count // fold
    return jnp.concatenate(
        [
            ref[row : row + rows, col + i * width : col + (i + 1) * width]
            for i in range(fold)
        ],
        0,
    )


def folded_rows(count, width, points):
    return count // min(points // width, count // 16)


def call(body, outs, args, flops, vmem=12, scratch=(), hbm=()):
    spec = pl.BlockSpec(memory_space=pltpu.VMEM)
    anywhere = pl.BlockSpec(memory_space=pltpu.HBM)
    size = sum(int(np.prod(a.shape)) * a.dtype.itemsize for a in args)
    return pl.pallas_call(
        body,
        out_shape=outs,
        in_specs=[anywhere if i in hbm else spec for i in range(len(args))],
        out_specs=[spec] * len(outs),
        scratch_shapes=list(scratch),
        cost_estimate=pl.CostEstimate(flops=flops, bytes_accessed=size, transcendentals=0),
        compiler_params=pltpu.CompilerParams(vmem_limit_bytes=vmem * MIB),
    )(*args)


def shape(*dims, dtype=BF):
    return jax.ShapeDtypeStruct(dims, dtype)


def local(propagator, incident, coeffs):
    weights = propagator[0]
    source = incident[0]
    coeffs = coeffs[0].T
    count, points = coeffs.shape
    nfreq, _, width = source.shape
    table = angle_table(count, points)
    panel = 2 * count
    rows = folded_rows(count, width, points)
    total = nfreq * rows
    spread = panel * (count // 16)
    near = points * count * panel * nfreq * 2
    whole = nfreq * 2 * points * points * panel * 2

    def swap(x, y):
        far = exchanged(y, "depth", 1)
        near = exchanged(x, "depth", 0)
        return near, far

    def from_below(near_ref, far_ref, low, high):
        return jnp.where(is_even("depth"), near_ref[low:high], far_ref[low:high])

    def from_above(near_ref, far_ref, low, high):
        return jnp.where(is_even("depth"), far_ref[low:high], near_ref[low:high])

    hbm = pltpu.HBM

    def first(s_ref, c_ref, t_ref, out, table_out, src, coef, sems):
        copies = [
            pltpu.make_async_copy(t_ref, table_out, sems.at[0]),
            pltpu.make_async_copy(c_ref, coef, sems.at[1]),
            pltpu.make_async_copy(s_ref, src, sems.at[2]),
        ]
        for copy in copies:
            copy.start()
        copies[0].wait()
        copies[1].wait()
        out[0:count] = (coef[...] * table_out[...].astype(F32)).astype(BF)
        copies[2].wait()
        for f in range(nfreq):
            pack(out, count + f * rows, 0, dot(table_out[...], src[f]).astype(BF))

    own1, table = call(
        first,
        [shape(count + total, points), pltpu.VMEM((count, points), BF)],
        [pltpu.with_memory_space_constraint(x, hbm) for x in (source, coeffs, table)],
        near,
        scratch=[
            pltpu.VMEM(source.shape, BF),
            pltpu.VMEM(coeffs.shape, F32),
            pltpu.SemaphoreType.DMA((3,)),
        ],
        hbm=(0, 1, 2),
    )
    near1, far1 = swap(own1, own1)

    def load(w_ref, t_ref, kept, seen, sems):
        copies = [
            pltpu.make_async_copy(w_ref.at[f, c], kept.at[f, c], sems.at[2 * f + c])
            for f in range(nfreq)
            for c in range(2)
        ]
        for copy in copies:
            copy.start()
        for f in range(nfreq):
            for c in range(2):
                copies[2 * f + c].wait()
                seen[f, c * count : (c + 1) * count] = dot(t_ref[...], kept[f, c]).astype(BF)

    kept, seen = call(
        load,
        [pltpu.VMEM(weights.shape, BF), shape(nfreq, panel, points)],
        [pltpu.with_memory_space_constraint(weights, hbm), table],
        whole // 2,
        scratch=[pltpu.SemaphoreType.DMA((2 * nfreq,))],
        hbm=(0,),
    )
    body = nfreq * panel

    def make_m(w_ref, t_ref, near_ref, far_ref, out, tm):
        kernel = from_below(near_ref, far_ref, 0, count)
        for f in range(nfreq):
            for c in range(2):
                row = f * panel + c * count
                out[row : row + count] = dot(kernel, w_ref[f, c]).astype(BF)
        out[body : body + total] = from_below(near_ref, far_ref, count, count + total)
        for f in range(nfreq):
            pair = dot_t(t_ref[...], out[f * panel : (f + 1) * panel]).astype(BF)
            tm[f] = pair
            start1 = unpack(out, body + f * rows, 0, count, width)
            pack(out, body + total + f * rows, 0, dot(pair, both(start1)).astype(BF))

    own2, tm = call(
        make_m,
        [shape(body + 2 * total, points), shape(nfreq, count, panel)],
        [kept, table, near1, far1],
        whole // 2,
    )
    near2, far2 = swap(own2, own2)

    def make_j(w_ref, near_ref, far_ref, s_ref, own_ref, out, g_out):
        kernel = from_above(near_ref, far_ref, 0, count)
        zero = jnp.zeros((count, points), BF)
        left = jnp.concatenate([kernel, zero], 0)
        right = jnp.concatenate([zero, kernel], 0)
        for f in range(nfreq):
            for c in range(2):
                row = f * panel + c * count
                out[row : row + count] = dot_t(kernel, w_ref[f, c]).astype(BF)
            g_out[f] = (
                dot_t(s_ref[f, 0:count], left) + dot_t(s_ref[f, count:panel], right)
            ).astype(BF)

    j, g = call(
        make_j,
        [shape(body, points), shape(nfreq, count, panel)],
        [kept, near1, far1, seen, own2],
        whole // 2,
    )

    def advance(w_ref, x, f):
        y = jnp.concatenate([-x[count:], x[:count]], 0)
        return (dot(x, w_ref[f, 0]) + dot(y, w_ref[f, 1])).astype(BF)

    def make_n(w_ref, t_ref, near_ref, far_ref, own_ref, tm_ref, j_ref, g_ref, out, x_out, y_out):
        for f in range(nfreq):
            m = from_below(near_ref, far_ref, f * panel, (f + 1) * panel)
            out[f * panel : (f + 1) * panel] = advance(w_ref, m, f)
        out[body : body + total] = from_below(near_ref, far_ref, body, body + total)

        def fill(up, down):
            up[0 : body + total] = out[...]
            down[0:body] = j_ref[...]
            down[body : body + total] = from_above(
                near_ref, far_ref, body + total, body + 2 * total
            )
            for f in range(nfreq):
                pack(up, body + total, f * spread, g_ref[f])
                pair = dot_t(t_ref[...], out[f * panel : (f + 1) * panel]).astype(BF)
                start1 = unpack(own_ref, body + f * rows, 0, count, width)
                start2 = unpack(out, body + f * rows, 0, count, width)
                value = dot(pair, both(start2)) + dot(tm_ref[f], both(start1))
                pack(down, body + total + f * rows, 0, value.astype(BF))

        @pl.when(is_even("depth"))
        def _():
            fill(y_out, x_out)

        @pl.when(jnp.logical_not(is_even("depth")))
        def _():
            fill(x_out, y_out)

    own3, x3, y3 = call(
        make_n,
        [
            shape(body + total, points),
            shape(body + 2 * total, points),
            shape(body + 2 * total, points),
        ],
        [kept, table, near2, far2, own2, tm, j, g],
        whole,
    )
    near3, far3 = swap(x3, y3)

    scale = float(1.0 / np.sqrt(np.float32(width // 2 * nfreq * lax.axis_size("freq"))))

    def make_q(
        w_ref, near_ref, far_ref, n_ref, m_ref, s_ref, g_ref, o_ref, q_out, f_out, c_out, a_out
    ):
        partial = jnp.zeros((count, points), F32)
        tail = from_below(near_ref, far_ref, body, body + 2 * total)
        above = from_above(near_ref, far_ref, body, body + 2 * total)
        for f in range(nfreq):
            j = from_above(near_ref, far_ref, f * panel, (f + 1) * panel)
            real = dot_t(s_ref[f, 0:count], j)
            imag = dot_t(s_ref[f, count:panel], j)
            h = (real + turned(imag)).astype(BF)
            tu1_two = unpack(above, f * rows, 0, count, width)
            tu2_one = unpack(above, total + f * rows, 0, count, width)
            down3 = dot(h, both(tu1_two)) + dot(g_ref[f], both(tu2_one))
            start = unpack(o_ref, count + f * rows, 0, count, width)
            angles = (start.astype(F32) - down3).astype(BF)
            a_out[f] = angles

            n = from_below(near_ref, far_ref, f * panel, (f + 1) * panel)
            q = advance(w_ref, n, f)
            q_out[f] = q
            low = body + f * rows
            start1 = unpack(m_ref, low, 0, count, width)
            start2 = unpack(n_ref, low, 0, count, width)
            start3 = unpack(tail, f * rows, 0, count, width)
            turn = unpack(tail, total, f * spread, count, panel)
            down2 = dot(turn, both(unpack(m_ref, low + total, 0, count, width)))
            shifted = (start1.astype(F32) - down2).astype(BF)
            fields = jnp.concatenate([both(start3), both(start2), both(shifted)], 0)
            f_out[f] = fields
            weight = dot_t(angles, fields).astype(BF)
            stack = jnp.concatenate(
                [q, n_ref[f * panel : (f + 1) * panel], m_ref[f * panel : (f + 1) * panel]], 0
            )
            partial = partial + dot(weight, stack)
        c_out[...] = (partial * scale).astype(BF)

    q, fields, partial, angles = call(
        make_q,
        [
            shape(nfreq, panel, points),
            shape(nfreq, 3 * panel, width),
            shape(count, points),
            shape(nfreq, count, width),
        ],
        [kept, near3, far3, own3, own2, seen, g, own1],
        whole + 5 * near,
    )

    def make_up(q_ref, n_ref, m_ref, f_ref, out):
        for f in range(nfreq):
            stack = jnp.concatenate(
                [
                    q_ref[f],
                    n_ref[f * panel : (f + 1) * panel],
                    m_ref[f * panel : (f + 1) * panel],
                ],
                0,
            )
            out[f] = t_dot(stack, f_ref[f]).astype(BF)

    (upgoing,) = call(
        make_up, [shape(nfreq, points, width)], [q, own3, own2, fields], 3 * near
    )

    size = lax.axis_size("freq")
    share = points // size
    value = partial
    steps = [step for step in (4, 1, 3) if step < size]
    for step in steps:
        other = lax.ppermute(value, "freq", [(i, i ^ step) for i in range(size)])
        if step != steps[-1]:
            value = (value.astype(F32) + other.astype(F32)).astype(BF)

    def last(c_ref, t_ref, v_ref, o_ref, a_ref, out, g_out, keep):
        gradient = v_ref[...].astype(F32) + o_ref[...].astype(F32)
        keep[...] = gradient
        kernel = ((c_ref[...] - gradient) * t_ref[...].astype(F32)).astype(BF)
        for f in range(nfreq):
            out[f] = t_dot(kernel, a_ref[f]).astype(BF)
        begin = pl.multiple_of(lax.axis_index("freq") * share, share)
        g_out[...] = keep[:, pl.ds(begin, share)]

    reflected, mine = call(
        last,
        [shape(nfreq, points, width), shape(count, share, dtype=F32)],
        [coeffs, table, value, other, angles],
        near,
        scratch=[pltpu.VMEM((count, points), F32)],
    )
    return (upgoing[None], mine.T[None], reflected[None])


def solution(mesh):
    return jax.shard_map(
        local,
        mesh=mesh,
        in_specs=(
            P("depth", "freq", None, None, None),
            P("depth", "freq", None, None),
            P("depth", None, None),
        ),
        out_specs=(
            P("depth", "freq", None, None),
            P("depth", "freq", None),
            P("depth", "freq", None, None),
        ),
        check_vma=False,
    )
```

time: 196 us -> 70.4 us (0.36)
  matrix products: 52.6 us -> 0 us
  waiting for transfers between devices: 55 us -> 24.9 us
  blocking collectives: 23.8 us -> 0 us
  Pallas kernels: 0 us -> 18.3 us
  local copies, waits for them, and re-layouts: 14.5 us -> 0.01 us
  between operations: 14.4 us -> 0.78 us
  other arithmetic: 5.72 us -> 0.07 us
  starting transfers between devices: 28.7 us -> 26.2 us
    dot_general x20 -> x0, matrix products: 52.6 us -> none  [the longest x6 20.7 us: apply_level(): jnp.einsum(form, weights[:, 1], field, preferred_element_type=jnp.float32)]
    unnamed x2 -> x0, waiting for transfers between devices: 36.8 us -> none
    all_gather x1 -> x0, blocking collectives: 23.8 us -> none  [local(): lax.all_gather(mine.astype(jnp.bfloat16), 'freq', axis=0, tiled=True)]
    pallas_call x0 -> x8, Pallas kernels: none -> 18.3 us  [call(): pl.pallas_call(body, out_shape=outs, in_specs=[anywhere if i in hbm else...]
    unnamed x22 -> x2, local copies, waits for them, and re-layouts: 14.5 us -> 0.01 us
    ppermute x6 -> x9, waiting for transfers between devices: 18.3 us -> 24.9 us  [the longest x6 15.2 us: exchanged(): return lax.ppermute(block, axis, route)]
    convert_element_type x2, other arithmetic: 2.73 us -> 0.07 us  [local(): value = (value.astype(F32) + other.astype(F32)).astype(BF)]
    ppermute x6 -> x9, starting transfers between devices: 28.7 us -> 26.2 us  [the longest x6 21.3 us: exchanged(): return lax.ppermute(block, axis, route)]
  transfers between devices with their start and end apart: 7 -> 9, of which waited for: 6 -> 5; matrix products, arithmetic and copies ran while one was open for 15% -> 0% of each run, Pallas kernels for 0% -> 12%
where the time goes in v2:
time: 70.4 us; the launch traced here: 70.2 us
  starting transfers between devices  26.2 us (37%)
  waiting for transfers between devices  24.9 us (35%)
  Pallas kernels  18.3 us (26%)
  between operations  0.78 us (1%)
    ppermute x6, starting transfers between devices, exchanged(): return lax.ppermute(block, axis, route)  21.3 us
    pallas_call x8, Pallas kernels, call(): pl.pallas_call(body, out_shape=outs, in_specs=[anywhere if i in hbm else...  18.3 us
    ppermute x6, waiting for transfers between devices, exchanged(): return lax.ppermute(block, axis, route)  15.2 us
    ppermute x3, waiting for transfers between devices, local(): other = lax.ppermute(value, 'freq', [(i, i ^ step) for i in range(size)])  9.74 us
    ppermute x3, starting transfers between devices, local(): other = lax.ppermute(value, 'freq', [(i, i ^ step) for i in range(size)])  4.86 us
  transfers between devices with their start and end apart: 9, of which 5 were waited for; matrix products, arithmetic and copies ran while one was open for 0% of the time, Pallas kernels for 12%

profile of v2, /device:TPU:6, one launch (start us, length us, event | category | flops | bytes accessed | tf_op | source)
XLA Modules:
  0.0 70.2 jit_solution(13040638027937078687)
XLA Ops:
  0.6 1.7 %shard_map.67 = (bf16[96,1024]{1,0:T(8,128)(2,1)S(1)}, bf16[64,1024]{1,0:T(8,128)(2,1)S(1)}) custom-call(bf16[2,1024,256]{2,1,0:T(8,128)(2,1)} %bitcast.14, f32[64,1024]{1,0:T(8,128)} %bitcast.10, bf16[64,1024]{1,0:T(8,128)(2,1)} %constant.2.clone.t_ref), custom_call_target="tpu_custom_call" | custom-call | flops 33554432 | bytes 1441792 | tf_op jit(solution)/shard_map/pallas_call | solution.py:84
  2.3 8.0 %collective-permute-start.1 = (bf16[96,1024]{1,0:T(8,128)(2,1)S(1)}, bf16[96,1024]{1,0:T(8,128)(2,1)S(1)}, u32[]{:S(2)}, u32[]{:S(2)}) collective-permute-start(bf16[96,1024]{1,0:T(8,128)(2,1)S(1)} %get-tuple-element.22.o_ref), channel_id=1, source_target_pairs={{8,16},{16,8},{24,32},{32,24},{40,48},{48,40},{56,64},{64,56},{72,... | collective-permute-start | bytes 589832 | tf_op jit(solution)/shard_map/ppermute | solution.py:19
  10.4 0.1 collective-permute-start
  10.5 4.0 %shard_map.68 = (bf16[2,2,1024,1024]{3,2,1,0:T(8,128)(2,1)S(1)}, bf16[2,128,1024]{2,1,0:T(8,128)(2,1)S(1)}) custom-call(bf16[2,2,1024,1024]{3,2,1,0:T(8,128)(2,1)} %bitcast.12, bf16[64,1024]{1,0:T(8,128)(2,1)S(1)} %get-tuple-element.20.t_ref), custom_call_target="tpu_custom_call" | custom-call | flops 536870912 | bytes 8519680 | tf_op jit(solution)/shard_map/pallas_call | solution.py:84
  14.5 0.0 collective-permute-done.1.far_ref
  14.5 0.0 collective-permute-done.near_ref
  14.5 2.1 %shard_map.69 = (bf16[320,1024]{1,0:T(8,128)(2,1)S(1)}, bf16[2,64,128]{2,1,0:T(8,128)(2,1)S(1)}) custom-call(bf16[2,2,1024,1024]{3,2,1,0:T(8,128)(2,1)S(1)} %get-tuple-element.21.w_ref, bf16[64,1024]{1,0:T(8,128)(2,1)S(1)} %get-tuple-element.20.t_ref, bf16[96,1024]{1,0:T(8,128)(2,1)S(1)} %collective-permute-done.near_ref, ...), custom_call_target="tpu_custom_call" | custom-call | flops 536870912 | bytes 8912896 | tf_op jit(solution)/shard_map/pallas_call | solution.py:84
  16.6 6.5 %collective-permute-start.3 = (bf16[320,1024]{1,0:T(8,128)(2,1)S(1)}, bf16[320,1024]{1,0:T(8,128)(2,1)S(1)}, u32[]{:S(2)}, u32[]{:S(2)}) collective-permute-start(bf16[320,1024]{1,0:T(8,128)(2,1)S(1)} %get-tuple-element.23.own_ref.m_ref), channel_id=1, source_target_pairs={{8,16},{16,8},{24,32},{32,24},{40,48},{48,40},{56,64},{64,56},{72,... | collective-permute-start | bytes 1966088 | tf_op jit(solution)/shard_map/ppermute | solution.py:19
  23.1 0.1 collective-permute-start.2
  23.2 2.9 %shard_map.70 = (bf16[256,1024]{1,0:T(8,128)(2,1)S(1)}, bf16[2,64,128]{2,1,0:T(8,128)(2,1)S(1)}) custom-call(bf16[2,2,1024,1024]{3,2,1,0:T(8,128)(2,1)S(1)} %get-tuple-element.21.w_ref, bf16[96,1024]{1,0:T(8,128)(2,1)S(1)} %collective-permute-done.near_ref, bf16[96,1024]{1,0:T(8,128)(2,1)S(1)} %collective-permute-done.1.far_ref, ...), custom_call_target="tpu_custom_call" | custom-call | flops 536870912 | bytes 9961472 | tf_op jit(solution)/shard_map/pallas_call | solution.py:84
  26.1 6.1 %collective-permute-done.3.far_ref = bf16[320,1024]{1,0:T(8,128)(2,1)S(1)} collective-permute-done((bf16[320,1024]{1,0:T(8,128)(2,1)S(1)}, bf16[320,1024]{1,0:T(8,128)(2,1)S(1)}, u32[]{:S(2)}, u32[]{:S(2)}) %collective-permute-start.3) | collective-permute-done | bytes 655392 | tf_op jit(solution)/shard_map/ppermute | solution.py:19
  32.1 0.0 collective-permute-done.2.near_ref
  32.1 2.0 %shard_map.71 = (bf16[288,1024]{1,0:T(8,128)(2,1)S(1)}, bf16[320,1024]{1,0:T(8,128)(2,1)S(1)}, bf16[320,1024]{1,0:T(8,128)(2,1)S(1)}) custom-call(bf16[2,2,1024,1024]{3,2,1,0:T(8,128)(2,1)S(1)} %get-tuple-element.21.w_ref, bf16[64,1024]{1,0:T(8,128)(2,1)S(1)} %get-tuple-element.20.t_ref, bf16[320,1024]{1,0:T(8,128)(2,1)S(1)} %collective-permute-done.2.near_ref, ...), custom_call_target="tpu_custom_call" | custom-call | flops 1073741824 | bytes 11075584 | tf_op jit(solution)/shard_map/pallas_call | solution.py:84
  34.1 0.0 copy-start
  34.1 0.1 collective-permute-start.4
  34.2 6.5 %collective-permute-start.5 = (bf16[320,1024]{1,0:T(8,128)(2,1)S(1)}, bf16[320,1024]{1,0:T(8,128)(2,1)S(1)}, u32[]{:S(2)}, u32[]{:S(2)}) collective-permute-start(bf16[320,1024]{1,0:T(8,128)(2,1)S(1)} %get-tuple-element.29), channel_id=1, source_target_pairs={{8,16},{16,8},{24,32},{32,24},{40,48},{48,40},{56,64},{64,56},{72,... | collective-permute-start | bytes 1966088 | tf_op jit(solution)/shard_map/ppermute | solution.py:19
  40.7 0.0 collective-permute-done.4.near_ref
  40.8 9.1 %collective-permute-done.5.far_ref = bf16[320,1024]{1,0:T(8,128)(2,1)S(1)} collective-permute-done((bf16[320,1024]{1,0:T(8,128)(2,1)S(1)}, bf16[320,1024]{1,0:T(8,128)(2,1)S(1)}, u32[]{:S(2)}, u32[]{:S(2)}) %collective-permute-start.5) | collective-permute-done | bytes 655392 | tf_op jit(solution)/shard_map/ppermute | solution.py:19
  49.9 2.4 %shard_map.72 = (bf16[2,128,1024]{2,1,0:T(8,128)(2,1)S(1)}, bf16[2,384,256]{2,1,0:T(8,128)(2,1)S(1)}, bf16[64,1024]{1,0:T(8,128)(2,1)S(1)}, bf16[2,64,256]{2,1,0:T(8,128)(2,1)S(1)}) custom-call(bf16[2,2,1024,1024]{3,2,1,0:T(8,128)(2,1)S(1)} %get-tuple-element.21.w_ref, bf16[320,1024]{1,0:T(8,128)(2,1)S(1)} %collective-permute-done.4.near_ref, ...), custom_call_target="tpu_custom_call" | custom-call | flops 1241513984 | bytes 11698176 | tf_op jit(solution)/shard_map/pallas_call | solution.py:84
  52.3 0.1 collective-permute-start.6
  52.4 5.0 %collective-permute-done.6 = bf16[64,1024]{1,0:T(8,128)(2,1)S(1)} collective-permute-done((bf16[64,1024]{1,0:T(8,128)(2,1)S(1)}, bf16[64,1024]{1,0:T(8,128)(2,1)S(1)}, u32[]{:S(2)}, u32[]{:S(2)}) %collective-permute-start.6) | collective-permute-done | bytes 131104 | tf_op jit(solution)/shard_map/ppermute | solution.py:335
  57.4 1.7 %collective-permute-start.7 = (bf16[64,1024]{1,0:T(8,128)(2,1)S(1)}, bf16[64,1024]{1,0:T(8,128)(2,1)S(1)}, u32[]{:S(2)}, u32[]{:S(2)}) collective-permute-start(bf16[64,1024]{1,0:T(8,128)(2,1)S(1)} %add_convert_fusion.1), channel_id=1, source_target_pairs={{0,1},{1,0},{2,3},{3,2},{4,5},{5,4},{6,7},{7,6},{8,9},{9,8},{10,11... | collective-permute-start | bytes 393224 | tf_op jit(solution)/shard_map/ppermute | solution.py:335
  59.0 3.4 %collective-permute-done.7 = bf16[64,1024]{1,0:T(8,128)(2,1)S(1)} collective-permute-done((bf16[64,1024]{1,0:T(8,128)(2,1)S(1)}, bf16[64,1024]{1,0:T(8,128)(2,1)S(1)}, u32[]{:S(2)}, u32[]{:S(2)}) %collective-permute-start.7) | collective-permute-done | bytes 131104 | tf_op jit(solution)/shard_map/ppermute | solution.py:335
  62.5 3.1 %collective-permute-start.8 = (bf16[64,1024]{1,0:T(8,128)(2,1)S(1)}, bf16[64,1024]{1,0:T(8,128)(2,1)S(1)}, u32[]{:S(2)}, u32[]{:S(2)}) collective-permute-start(bf16[64,1024]{1,0:T(8,128)(2,1)S(1)} %add_convert_fusion.v_ref), channel_id=1, source_target_pairs={{0,3},{1,2},{2,1},{3,0},{4,7},{5,6},{6,5},{7,4},{8,11},{9,10},{10,... | collective-permute-start | bytes 393224 | tf_op jit(solution)/shard_map/ppermute | solution.py:335
  65.6 1.8 %shard_map.73 = bf16[2,1024,256]{2,1,0:T(8,128)(2,1)} custom-call(bf16[2,128,1024]{2,1,0:T(8,128)(2,1)S(1)} %get-tuple-element.31.q_ref, bf16[288,1024]{1,0:T(8,128)(2,1)S(1)} %get-tuple-element.30.n_ref, bf16[320,1024]{1,0:T(8,128)(2,1)S(1)} %get-tuple-element.23.own_ref.m_ref, bf16[2,384,256]{2,1,0:T(8,128)(2,1)S(1)} %get-tuple-element.32.f_ref), custom_call_target="tpu_custom_call" | custom-call | flops 100663296 | bytes 2162688 | tf_op jit(solution)/shard_map/pallas_call | solution.py:84
  67.3 1.4 %collective-permute-done.8.o_ref = bf16[64,1024]{1,0:T(8,128)(2,1)S(1)} collective-permute-done((bf16[64,1024]{1,0:T(8,128)(2,1)S(1)}, bf16[64,1024]{1,0:T(8,128)(2,1)S(1)}, u32[]{:S(2)}, u32[]{:S(2)}) %collective-permute-start.8) | collective-permute-done | bytes 131104 | tf_op jit(solution)/shard_map/ppermute | solution.py:335
  68.7 0.0 copy-done
  68.7 1.4 %shard_map.74 = (bf16[2,1024,256]{2,1,0:T(8,128)(2,1)}, f32[64,128]{1,0:T(8,128)}) custom-call(f32[64,1024]{1,0:T(8,128)S(1)} %bitcast.11, bf16[64,1024]{1,0:T(8,128)(2,1)S(1)} %get-tuple-element.20.t_ref, bf16[64,1024]{1,0:T(8,128)(2,1)S(1)} %add_convert_fusion.v_ref, bf16[64,1024]{1,0:T(8,128)(2,1)S(1)} %collective-permute-done.8.o_ref, ...), custom_call_target="tpu_custom_call" | custom-call | flops 33554432 | bytes 720896 | tf_op jit(solution)/shard_map/pallas_call | solution.py:84
  (2 shorter events, 0.1 us)
Async XLA Ops:
  2.3 12.2 %collective-permute-start.1 = (bf16[96,1024]{1,0:T(8,128)(2,1)S(1)}, bf16[96,1024]{1,0:T(8,128)(2,1)S(1)}, u32[]{:S(2)}, u32[]{:S(2)}) collective-permute-start(bf16[96,1024]{1,0:T(8,128)(2,1)S(1)} %get-tuple-element.22.o_ref), channel_id=1, source_target_pairs={{8,16},{16,8},{24,32},{32,24},{40,48},{48,40},{56,64},{64,56},{72,... | collective-permute-start | bytes 589832 | tf_op jit(solution)/shard_map/ppermute | solution.py:19
  10.4 4.1 %collective-permute-start = (bf16[96,1024]{1,0:T(8,128)(2,1)S(1)}, bf16[96,1024]{1,0:T(8,128)(2,1)S(1)}, u32[]{:S(2)}, u32[]{:S(2)}) collective-permute-start(bf16[96,1024]{1,0:T(8,128)(2,1)S(1)} %get-tuple-element.22.o_ref), channel_id=1, source_target_pairs={{0,8},{8,0},{16,24},{24,16},{32,40},{40,32},{48,56},{56,48},{64,72... | collective-permute-start | bytes 589832 | tf_op jit(solution)/shard_map/ppermute | solution.py:19
  16.6 15.5 %collective-permute-start.3 = (bf16[320,1024]{1,0:T(8,128)(2,1)S(1)}, bf16[320,1024]{1,0:T(8,128)(2,1)S(1)}, u32[]{:S(2)}, u32[]{:S(2)}) collective-permute-start(bf16[320,1024]{1,0:T(8,128)(2,1)S(1)} %get-tuple-element.23.own_ref.m_ref), channel_id=1, source_target_pairs={{8,16},{16,8},{24,32},{32,24},{40,48},{48,40},{56,64},{64,56},{72,... | collective-permute-start | bytes 1966088 | tf_op jit(solution)/shard_map/ppermute | solution.py:19
  23.1 9.0 %collective-permute-start.2 = (bf16[320,1024]{1,0:T(8,128)(2,1)S(1)}, bf16[320,1024]{1,0:T(8,128)(2,1)S(1)}, u32[]{:S(2)}, u32[]{:S(2)}) collective-permute-start(bf16[320,1024]{1,0:T(8,128)(2,1)S(1)} %get-tuple-element.23.own_ref.m_ref), channel_id=1, source_target_pairs={{0,8},{8,0},{16,24},{24,16},{32,40},{40,32},{48,56},{56,48},{64,72... | collective-permute-start | bytes 1966088 | tf_op jit(solution)/shard_map/ppermute | solution.py:19
  34.1 34.6 %copy-start = (f32[1,1024,64]{1,2,0:T(8,128)S(1)}, f32[1,1024,64]{1,2,0:T(8,128)}, u32[]{:S(2)}) copy-start(f32[1,1024,64]{1,2,0:T(8,128)} %param.6) | copy-start | bytes 786436
  34.1 6.6 %collective-permute-start.4 = (bf16[320,1024]{1,0:T(8,128)(2,1)S(1)}, bf16[320,1024]{1,0:T(8,128)(2,1)S(1)}, u32[]{:S(2)}, u32[]{:S(2)}) collective-permute-start(bf16[320,1024]{1,0:T(8,128)(2,1)S(1)} %get-tuple-element.28), channel_id=1, source_target_pairs={{0,8},{8,0},{16,24},{24,16},{32,40},{40,32},{48,56},{56,48},{64,72... | collective-permute-start | bytes 1966088 | tf_op jit(solution)/shard_map/ppermute | solution.py:19
  34.2 15.6 %collective-permute-start.5 = (bf16[320,1024]{1,0:T(8,128)(2,1)S(1)}, bf16[320,1024]{1,0:T(8,128)(2,1)S(1)}, u32[]{:S(2)}, u32[]{:S(2)}) collective-permute-start(bf16[320,1024]{1,0:T(8,128)(2,1)S(1)} %get-tuple-element.29), channel_id=1, source_target_pairs={{8,16},{16,8},{24,32},{32,24},{40,48},{48,40},{56,64},{64,56},{72,... | collective-permute-start | bytes 1966088 | tf_op jit(solution)/shard_map/ppermute | solution.py:19
  52.3 5.1 %collective-permute-start.6 = (bf16[64,1024]{1,0:T(8,128)(2,1)S(1)}, bf16[64,1024]{1,0:T(8,128)(2,1)S(1)}, u32[]{:S(2)}, u32[]{:S(2)}) collective-permute-start(bf16[64,1024]{1,0:T(8,128)(2,1)S(1)} %get-tuple-element.33), channel_id=1, source_target_pairs={{0,4},{1,5},{2,6},{3,7},{4,0},{5,1},{6,2},{7,3},{8,12},{9,13},{10,... | collective-permute-start | bytes 393224 | tf_op jit(solution)/shard_map/ppermute | solution.py:335
  57.4 5.1 %collective-permute-start.7 = (bf16[64,1024]{1,0:T(8,128)(2,1)S(1)}, bf16[64,1024]{1,0:T(8,128)(2,1)S(1)}, u32[]{:S(2)}, u32[]{:S(2)}) collective-permute-start(bf16[64,1024]{1,0:T(8,128)(2,1)S(1)} %add_convert_fusion.1), channel_id=1, source_target_pairs={{0,1},{1,0},{2,3},{3,2},{4,5},{5,4},{6,7},{7,6},{8,9},{9,8},{10,11... | collective-permute-start | bytes 393224 | tf_op jit(solution)/shard_map/ppermute | solution.py:335
  62.5 6.3 %collective-permute-start.8 = (bf16[64,1024]{1,0:T(8,128)(2,1)S(1)}, bf16[64,1024]{1,0:T(8,128)(2,1)S(1)}, u32[]{:S(2)}, u32[]{:S(2)}) collective-permute-start(bf16[64,1024]{1,0:T(8,128)(2,1)S(1)} %add_convert_fusion.v_ref), channel_id=1, source_target_pairs={{0,3},{1,2},{2,1},{3,0},{4,7},{5,6},{6,5},{7,4},{8,11},{9,10},{10,... | collective-permute-start | bytes 393224 | tf_op jit(solution)/shard_map/ppermute | solution.py:335

commit v3 on v2

--- a/solution.py
+++ b/solution.py
@@ -175,28 +175,28 @@
     )
     body = nfreq * panel
 
+    height = body + total + 16
+
     def make_m(w_ref, t_ref, near_ref, far_ref, out, tm):
         kernel = from_below(near_ref, far_ref, 0, count)
-        for f in range(nfreq):
-            for c in range(2):
-                row = f * panel + c * count
-                out[row : row + count] = dot(kernel, w_ref[f, c]).astype(BF)
         out[body : body + total] = from_below(near_ref, far_ref, count, count + total)
         for f in range(nfreq):
-            pair = dot_t(t_ref[...], out[f * panel : (f + 1) * panel]).astype(BF)
+            parts = [dot(kernel, w_ref[f, c]).astype(BF) for c in range(2)]
+            m = jnp.concatenate(parts, 0)
+            out[f * panel : (f + 1) * panel] = m
+            pair = dot_t(t_ref[...], m).astype(BF)
             tm[f] = pair
-            start1 = unpack(out, body + f * rows, 0, count, width)
-            pack(out, body + total + f * rows, 0, dot(pair, both(start1)).astype(BF))
+            pack(out, body + total, f * spread, pair)
 
     own2, tm = call(
         make_m,
-        [shape(body + 2 * total, points), shape(nfreq, count, panel)],
+        [shape(height, points), shape(nfreq, count, panel)],
         [kept, table, near1, far1],
         whole // 2,
     )
     near2, far2 = swap(own2, own2)
 
-    def make_j(w_ref, near_ref, far_ref, s_ref, own_ref, out, g_out):
+    def make_j(w_ref, near_ref, far_ref, s_ref, own_ref, tm_ref, out, g_out, u_out):
         kernel = from_above(near_ref, far_ref, 0, count)
         zero = jnp.zeros((count, points), BF)
         left = jnp.concatenate([kernel, zero], 0)
@@ -208,11 +208,17 @@
             g_out[f] = (
                 dot_t(s_ref[f, 0:count], left) + dot_t(s_ref[f, count:panel], right)
             ).astype(BF)
-
-    j, g = call(
+            start1 = unpack(own_ref, body + f * rows, 0, count, width)
+            u_out[f] = dot(tm_ref[f], both(start1)).astype(BF)
+
+    j, g, tu1 = call(
         make_j,
-        [shape(body, points), shape(nfreq, count, panel)],
-        [kept, near1, far1, seen, own2],
+        [
+            shape(body, points),
+            shape(nfreq, count, panel),
+            shape(nfreq, count, width),
+        ],
+        [kept, near1, far1, seen, own2, tm],
         whole // 2,
     )
 
@@ -220,42 +226,46 @@
         y = jnp.concatenate([-x[count:], x[:count]], 0)
         return (dot(x, w_ref[f, 0]) + dot(y, w_ref[f, 1])).astype(BF)
 
-    def make_n(w_ref, t_ref, near_ref, far_ref, own_ref, tm_ref, j_ref, g_ref, out, x_out, y_out):
-        for f in range(nfreq):
-            m = from_below(near_ref, far_ref, f * panel, (f + 1) * panel)
-            out[f * panel : (f + 1) * panel] = advance(w_ref, m, f)
-        out[body : body + total] = from_below(near_ref, far_ref, body, body + total)
-
-        def fill(up, down):
-            up[0 : body + total] = out[...]
-            down[0:body] = j_ref[...]
-            down[body : body + total] = from_above(
-                near_ref, far_ref, body + total, body + 2 * total
-            )
-            for f in range(nfreq):
-                pack(up, body + total, f * spread, g_ref[f])
-                pair = dot_t(t_ref[...], out[f * panel : (f + 1) * panel]).astype(BF)
-                start1 = unpack(own_ref, body + f * rows, 0, count, width)
-                start2 = unpack(out, body + f * rows, 0, count, width)
-                value = dot(pair, both(start2)) + dot(tm_ref[f], both(start1))
-                pack(down, body + total + f * rows, 0, value.astype(BF))
-
-        @pl.when(is_even("depth"))
-        def _():
-            fill(y_out, x_out)
-
-        @pl.when(jnp.logical_not(is_even("depth")))
-        def _():
-            fill(x_out, y_out)
-
-    own3, x3, y3 = call(
+    def make_n(w_ref, t_ref, near_ref, far_ref, o_ref, j_ref, g_ref, out, x_out, y_out, u_out):
+        even = is_even("depth")
+        low = body + total
+
+        def put(row, col, up, down):
+            place = (slice(row, row + up.shape[0]), slice(col, col + up.shape[1]))
+            x_out[place] = jnp.where(even, down, up)
+            y_out[place] = jnp.where(even, up, down)
+
+        angles = from_below(near_ref, far_ref, body, low)
+        out[body:] = angles
+        above = from_above(near_ref, far_ref, low, height)
+        for f in range(nfreq):
+            first_row = f * panel
+            x = from_below(near_ref, far_ref, first_row, first_row + panel)
+            n = advance(w_ref, x, f)
+            out[first_row : first_row + panel] = n
+            put(first_row, 0, n, j_ref[first_row : first_row + panel])
+            pair = dot_t(t_ref[...], n).astype(BF)
+            for i in range(count // 16):
+                cut = slice(i * 16, (i + 1) * 16)
+                put(low, f * spread + i * panel, g_ref[f, cut], pair[cut])
+            start = unpack(o_ref, count + f * rows, 0, count, width)
+            pair_above = unpack(above, 0, f * spread, count, panel)
+            seen_above = dot(pair_above, both(start)).astype(BF)
+            u_out[f] = seen_above
+            for i in range(count // rows):
+                cut = slice(i * rows, (i + 1) * rows)
+                up = angles[f * rows : (f + 1) * rows, i * width : (i + 1) * width]
+                put(body + f * rows, i * width, up, seen_above[cut])
+
+    own3, x3, y3, tu1_above = call(
         make_n,
         [
             shape(body + total, points),
-            shape(body + 2 * total, points),
-            shape(body + 2 * total, points),
-        ],
-        [kept, table, near2, far2, own2, tm, j, g],
+            shape(height, points),
+            shape(height, points),
+            shape(nfreq, count, width),
+        ],
+        [kept, table, near2, far2, own1, j, g],
         whole,
     )
     near3, far3 = swap(x3, y3)
@@ -263,18 +273,22 @@
     scale = float(1.0 / np.sqrt(np.float32(width // 2 * nfreq * lax.axis_size("freq"))))
 
     def make_q(
-        w_ref, near_ref, far_ref, n_ref, m_ref, s_ref, g_ref, o_ref, q_out, f_out, c_out, a_out
+        w_ref, near_ref, far_ref, n_ref, m_ref, s_ref, g_ref, o_ref, u_ref, v_ref,
+        q_out, f_out, c_out, a_out
     ):
         partial = jnp.zeros((count, points), F32)
-        tail = from_below(near_ref, far_ref, body, body + 2 * total)
-        above = from_above(near_ref, far_ref, body, body + 2 * total)
+        tail = from_below(near_ref, far_ref, body, height)
+        above = from_above(near_ref, far_ref, body, height)
         for f in range(nfreq):
             j = from_above(near_ref, far_ref, f * panel, (f + 1) * panel)
             real = dot_t(s_ref[f, 0:count], j)
             imag = dot_t(s_ref[f, count:panel], j)
             h = (real + turned(imag)).astype(BF)
             tu1_two = unpack(above, f * rows, 0, count, width)
-            tu2_one = unpack(above, total + f * rows, 0, count, width)
+            low = body + f * rows
+            start1 = unpack(m_ref, low, 0, count, width)
+            pair = unpack(above, total, f * spread, count, panel)
+            tu2_one = (dot(pair, both(start1)) + v_ref[f].astype(F32)).astype(BF)
             down3 = dot(h, both(tu1_two)) + dot(g_ref[f], both(tu2_one))
             start = unpack(o_ref, count + f * rows, 0, count, width)
             angles = (start.astype(F32) - down3).astype(BF)
@@ -283,12 +297,10 @@
             n = from_below(near_ref, far_ref, f * panel, (f + 1) * panel)
             q = advance(w_ref, n, f)
             q_out[f] = q
-            low = body + f * rows
-            start1 = unpack(m_ref, low, 0, count, width)
             start2 = unpack(n_ref, low, 0, count, width)
             start3 = unpack(tail, f * rows, 0, count, width)
             turn = unpack(tail, total, f * spread, count, panel)
-            down2 = dot(turn, both(unpack(m_ref, low + total, 0, count, width)))
+            down2 = dot(turn, both(u_ref[f]))
             shifted = (start1.astype(F32) - down2).astype(BF)
             fields = jnp.concatenate([both(start3), both(start2), both(shifted)], 0)
             f_out[f] = fields
@@ -307,7 +319,7 @@
             shape(count, points),
             shape(nfreq, count, width),
         ],
-        [kept, near3, far3, own3, own2, seen, g, own1],
+        [kept, near3, far3, own3, own2, seen, g, own1, tu1, tu1_above],
         whole + 5 * near,
     )
 

time: 70.4 us -> 69.1 us (0.982)
  no operation moved by 1% of the time
where the time goes in v3:
time: 69.1 us; the launch traced here: 68.9 us
  starting transfers between devices  26.1 us (38%)
  waiting for transfers between devices  24.3 us (35%)
  Pallas kernels  17.6 us (25%)
  between operations  0.78 us (1%)
    ppermute x6, starting transfers between devices, exchanged(): return lax.ppermute(block, axis, route)  21.3 us
    pallas_call x8, Pallas kernels, call(): pl.pallas_call(body, out_shape=outs, in_specs=[anywhere if i in hbm else...  17.6 us
    ppermute x6, waiting for transfers between devices, exchanged(): return lax.ppermute(block, axis, route)  14.6 us
    ppermute x3, waiting for transfers between devices, local(): other = lax.ppermute(value, 'freq', [(i, i ^ step) for i in range(size)])  9.75 us
    ppermute x3, starting transfers between devices, local(): other = lax.ppermute(value, 'freq', [(i, i ^ step) for i in range(size)])  4.85 us
  transfers between devices with their start and end apart: 9, of which 5 were waited for; matrix products, arithmetic and copies ran while one was open for 0% of the time, Pallas kernels for 12%

profile of v3, /device:TPU:6, one launch (start us, length us, event | category | flops | bytes accessed | tf_op | source)
XLA Modules:
  0.0 68.9 jit_solution(6021000696210929726)
XLA Ops:
  0.6 1.7 %shard_map.67 = (bf16[96,1024]{1,0:T(8,128)(2,1)S(1)}, bf16[64,1024]{1,0:T(8,128)(2,1)S(1)}) custom-call(bf16[2,1024,256]{2,1,0:T(8,128)(2,1)} %bitcast.14, f32[64,1024]{1,0:T(8,128)} %bitcast.10, bf16[64,1024]{1,0:T(8,128)(2,1)} %constant.2.clone.t_ref), custom_call_target="tpu_custom_call" | custom-call | flops 33554432 | bytes 1441792 | tf_op jit(solution)/shard_map/pallas_call | solution.py:84
  2.3 8.0 %collective-permute-start.1 = (bf16[96,1024]{1,0:T(8,128)(2,1)S(1)}, bf16[96,1024]{1,0:T(8,128)(2,1)S(1)}, u32[]{:S(2)}, u32[]{:S(2)}) collective-permute-start(bf16[96,1024]{1,0:T(8,128)(2,1)S(1)} %get-tuple-element.24.o_ref), channel_id=1, source_target_pairs={{8,16},{16,8},{24,32},{32,24},{40,48},{48,40},{56,64},{64,56},{72,... | collective-permute-start | bytes 589832 | tf_op jit(solution)/shard_map/ppermute | solution.py:19
  10.4 0.1 collective-permute-start
  10.5 4.0 %shard_map.68 = (bf16[2,2,1024,1024]{3,2,1,0:T(8,128)(2,1)S(1)}, bf16[2,128,1024]{2,1,0:T(8,128)(2,1)S(1)}) custom-call(bf16[2,2,1024,1024]{3,2,1,0:T(8,128)(2,1)} %bitcast.12, bf16[64,1024]{1,0:T(8,128)(2,1)S(1)} %get-tuple-element.22.t_ref), custom_call_target="tpu_custom_call" | custom-call | flops 536870912 | bytes 8519680 | tf_op jit(solution)/shard_map/pallas_call | solution.py:84
  14.5 0.0 collective-permute-done.1.far_ref
  14.5 0.0 collective-permute-done.near_ref
  14.5 1.9 %shard_map.69 = (bf16[304,1024]{1,0:T(8,128)(2,1)S(1)}, bf16[2,64,128]{2,1,0:T(8,128)(2,1)S(1)}) custom-call(bf16[2,2,1024,1024]{3,2,1,0:T(8,128)(2,1)S(1)} %get-tuple-element.23.w_ref, bf16[64,1024]{1,0:T(8,128)(2,1)S(1)} %get-tuple-element.22.t_ref, bf16[96,1024]{1,0:T(8,128)(2,1)S(1)} %collective-permute-done.near_ref, ...), custom_call_target="tpu_custom_call" | custom-call | flops 536870912 | bytes 8912896 | tf_op jit(solution)/shard_map/pallas_call | solution.py:84
  16.4 6.5 %collective-permute-start.3 = (bf16[304,1024]{1,0:T(8,128)(2,1)S(1)}, bf16[304,1024]{1,0:T(8,128)(2,1)S(1)}, u32[]{:S(2)}, u32[]{:S(2)}) collective-permute-start(bf16[304,1024]{1,0:T(8,128)(2,1)S(1)} %get-tuple-element.25.own_ref.m_ref), channel_id=1, source_target_pairs={{8,16},{16,8},{24,32},{32,24},{40,48},{48,40},{56,64},{64,56},{72,... | collective-permute-start | bytes 1867784 | tf_op jit(solution)/shard_map/ppermute | solution.py:19
  22.9 0.1 collective-permute-start.2
  23.0 2.7 %shard_map.70 = (bf16[256,1024]{1,0:T(8,128)(2,1)S(1)}, bf16[2,64,128]{2,1,0:T(8,128)(2,1)S(1)}, bf16[2,64,256]{2,1,0:T(8,128)(2,1)S(1)}) custom-call(bf16[2,2,1024,1024]{3,2,1,0:T(8,128)(2,1)S(1)} %get-tuple-element.23.w_ref, bf16[96,1024]{1,0:T(8,128)(2,1)S(1)} %collective-permute-done.near_ref, bf16[96,1024]{1,0:T(8,128)(2,1)S(1)} %collective-permute-done.1.far_ref, ...), custom_call_target="tpu_custom_call" | custom-call | flops 536870912 | bytes 9961472 | tf_op jit(solution)/shard_map/pallas_call | solution.py:84
  25.8 5.8 %collective-permute-done.3.far_ref = bf16[304,1024]{1,0:T(8,128)(2,1)S(1)} collective-permute-done((bf16[304,1024]{1,0:T(8,128)(2,1)S(1)}, bf16[304,1024]{1,0:T(8,128)(2,1)S(1)}, u32[]{:S(2)}, u32[]{:S(2)}) %collective-permute-start.3) | collective-permute-done | bytes 622624 | tf_op jit(solution)/shard_map/ppermute | solution.py:19
  31.6 0.0 collective-permute-done.2.near_ref
  31.6 1.6 %shard_map.71 = (bf16[288,1024]{1,0:T(8,128)(2,1)S(1)}, bf16[304,1024]{1,0:T(8,128)(2,1)S(1)}, bf16[304,1024]{1,0:T(8,128)(2,1)S(1)}, bf16[2,64,256]{2,1,0:T(8,128)(2,1)S(1)}) custom-call(bf16[2,2,1024,1024]{3,2,1,0:T(8,128)(2,1)S(1)} %get-tuple-element.23.w_ref, bf16[64,1024]{1,0:T(8,128)(2,1)S(1)} %get-tuple-element.22.t_ref, ...), custom_call_target="tpu_custom_call" | custom-call | flops 1073741824 | bytes 10518528 | tf_op jit(solution)/shard_map/pallas_call | solution.py:84
  33.2 0.0 copy-start
  33.2 0.1 collective-permute-start.4
  33.3 6.5 %collective-permute-start.5 = (bf16[304,1024]{1,0:T(8,128)(2,1)S(1)}, bf16[304,1024]{1,0:T(8,128)(2,1)S(1)}, u32[]{:S(2)}, u32[]{:S(2)}) collective-permute-start(bf16[304,1024]{1,0:T(8,128)(2,1)S(1)} %get-tuple-element.31), channel_id=1, source_target_pairs={{8,16},{16,8},{24,32},{32,24},{40,48},{48,40},{56,64},{64,56},{72,... | collective-permute-start | bytes 1867784 | tf_op jit(solution)/shard_map/ppermute | solution.py:19
  39.8 0.0 collective-permute-done.4.near_ref
  39.8 8.8 %collective-permute-done.5.far_ref = bf16[304,1024]{1,0:T(8,128)(2,1)S(1)} collective-permute-done((bf16[304,1024]{1,0:T(8,128)(2,1)S(1)}, bf16[304,1024]{1,0:T(8,128)(2,1)S(1)}, u32[]{:S(2)}, u32[]{:S(2)}) %collective-permute-start.5) | collective-permute-done | bytes 622624 | tf_op jit(solution)/shard_map/ppermute | solution.py:19
  48.6 2.4 %shard_map.72 = (bf16[2,128,1024]{2,1,0:T(8,128)(2,1)S(1)}, bf16[2,384,256]{2,1,0:T(8,128)(2,1)S(1)}, bf16[64,1024]{1,0:T(8,128)(2,1)S(1)}, bf16[2,64,256]{2,1,0:T(8,128)(2,1)S(1)}) custom-call(bf16[2,2,1024,1024]{3,2,1,0:T(8,128)(2,1)S(1)} %get-tuple-element.23.w_ref, bf16[304,1024]{1,0:T(8,128)(2,1)S(1)} %collective-permute-done.4.near_ref, ...), custom_call_target="tpu_custom_call" | custom-call | flops 1241513984 | bytes 11730944 | tf_op jit(solution)/shard_map/pallas_call | solution.py:84
  51.0 0.1 collective-permute-start.6
  51.1 5.0 %collective-permute-done.6 = bf16[64,1024]{1,0:T(8,128)(2,1)S(1)} collective-permute-done((bf16[64,1024]{1,0:T(8,128)(2,1)S(1)}, bf16[64,1024]{1,0:T(8,128)(2,1)S(1)}, u32[]{:S(2)}, u32[]{:S(2)}) %collective-permute-start.6) | collective-permute-done | bytes 131104 | tf_op jit(solution)/shard_map/ppermute | solution.py:347
  56.1 1.7 %collective-permute-start.7 = (bf16[64,1024]{1,0:T(8,128)(2,1)S(1)}, bf16[64,1024]{1,0:T(8,128)(2,1)S(1)}, u32[]{:S(2)}, u32[]{:S(2)}) collective-permute-start(bf16[64,1024]{1,0:T(8,128)(2,1)S(1)} %add_convert_fusion.1), channel_id=1, source_target_pairs={{0,1},{1,0},{2,3},{3,2},{4,5},{5,4},{6,7},{7,6},{8,9},{9,8},{10,11... | collective-permute-start | bytes 393224 | tf_op jit(solution)/shard_map/ppermute | solution.py:347
  57.8 3.4 %collective-permute-done.7 = bf16[64,1024]{1,0:T(8,128)(2,1)S(1)} collective-permute-done((bf16[64,1024]{1,0:T(8,128)(2,1)S(1)}, bf16[64,1024]{1,0:T(8,128)(2,1)S(1)}, u32[]{:S(2)}, u32[]{:S(2)}) %collective-permute-start.7) | collective-permute-done | bytes 131104 | tf_op jit(solution)/shard_map/ppermute | solution.py:347
  61.2 3.1 %collective-permute-start.8 = (bf16[64,1024]{1,0:T(8,128)(2,1)S(1)}, bf16[64,1024]{1,0:T(8,128)(2,1)S(1)}, u32[]{:S(2)}, u32[]{:S(2)}) collective-permute-start(bf16[64,1024]{1,0:T(8,128)(2,1)S(1)} %add_convert_fusion.v_ref), channel_id=1, source_target_pairs={{0,3},{1,2},{2,1},{3,0},{4,7},{5,6},{6,5},{7,4},{8,11},{9,10},{10,... | collective-permute-start | bytes 393224 | tf_op jit(solution)/shard_map/ppermute | solution.py:347
  64.3 1.8 %shard_map.73 = bf16[2,1024,256]{2,1,0:T(8,128)(2,1)} custom-call(bf16[2,128,1024]{2,1,0:T(8,128)(2,1)S(1)} %get-tuple-element.35.q_ref, bf16[288,1024]{1,0:T(8,128)(2,1)S(1)} %get-tuple-element.32.n_ref, bf16[304,1024]{1,0:T(8,128)(2,1)S(1)} %get-tuple-element.25.own_ref.m_ref, bf16[2,384,256]{2,1,0:T(8,128)(2,1)S(1)} %get-tuple-element.36.f_ref), custom_call_target="tpu_custom_call" | custom-call | flops 100663296 | bytes 2129920 | tf_op jit(solution)/shard_map/pallas_call | solution.py:84
  66.1 1.4 %collective-permute-done.8.o_ref = bf16[64,1024]{1,0:T(8,128)(2,1)S(1)} collective-permute-done((bf16[64,1024]{1,0:T(8,128)(2,1)S(1)}, bf16[64,1024]{1,0:T(8,128)(2,1)S(1)}, u32[]{:S(2)}, u32[]{:S(2)}) %collective-permute-start.8) | collective-permute-done | bytes 131104 | tf_op jit(solution)/shard_map/ppermute | solution.py:347
  67.5 0.0 copy-done
  67.5 1.4 %shard_map.74 = (bf16[2,1024,256]{2,1,0:T(8,128)(2,1)}, f32[64,128]{1,0:T(8,128)}) custom-call(f32[64,1024]{1,0:T(8,128)S(1)} %bitcast.11, bf16[64,1024]{1,0:T(8,128)(2,1)S(1)} %get-tuple-element.22.t_ref, bf16[64,1024]{1,0:T(8,128)(2,1)S(1)} %add_convert_fusion.v_ref, bf16[64,1024]{1,0:T(8,128)(2,1)S(1)} %collective-permute-done.8.o_ref, ...), custom_call_target="tpu_custom_call" | custom-call | flops 33554432 | bytes 720896 | tf_op jit(solution)/shard_map/pallas_call | solution.py:84
  (2 shorter events, 0.1 us)
Async XLA Ops:
  2.3 12.2 %collective-permute-start.1 = (bf16[96,1024]{1,0:T(8,128)(2,1)S(1)}, bf16[96,1024]{1,0:T(8,128)(2,1)S(1)}, u32[]{:S(2)}, u32[]{:S(2)}) collective-permute-start(bf16[96,1024]{1,0:T(8,128)(2,1)S(1)} %get-tuple-element.24.o_ref), channel_id=1, source_target_pairs={{8,16},{16,8},{24,32},{32,24},{40,48},{48,40},{56,64},{64,56},{72,... | collective-permute-start | bytes 589832 | tf_op jit(solution)/shard_map/ppermute | solution.py:19
  10.4 4.1 %collective-permute-start = (bf16[96,1024]{1,0:T(8,128)(2,1)S(1)}, bf16[96,1024]{1,0:T(8,128)(2,1)S(1)}, u32[]{:S(2)}, u32[]{:S(2)}) collective-permute-start(bf16[96,1024]{1,0:T(8,128)(2,1)S(1)} %get-tuple-element.24.o_ref), channel_id=1, source_target_pairs={{0,8},{8,0},{16,24},{24,16},{32,40},{40,32},{48,56},{56,48},{64,72... | collective-permute-start | bytes 589832 | tf_op jit(solution)/shard_map/ppermute | solution.py:19
  16.4 15.2 %collective-permute-start.3 = (bf16[304,1024]{1,0:T(8,128)(2,1)S(1)}, bf16[304,1024]{1,0:T(8,128)(2,1)S(1)}, u32[]{:S(2)}, u32[]{:S(2)}) collective-permute-start(bf16[304,1024]{1,0:T(8,128)(2,1)S(1)} %get-tuple-element.25.own_ref.m_ref), channel_id=1, source_target_pairs={{8,16},{16,8},{24,32},{32,24},{40,48},{48,40},{56,64},{64,56},{72,... | collective-permute-start | bytes 1867784 | tf_op jit(solution)/shard_map/ppermute | solution.py:19
  22.9 8.7 %collective-permute-start.2 = (bf16[304,1024]{1,0:T(8,128)(2,1)S(1)}, bf16[304,1024]{1,0:T(8,128)(2,1)S(1)}, u32[]{:S(2)}, u32[]{:S(2)}) collective-permute-start(bf16[304,1024]{1,0:T(8,128)(2,1)S(1)} %get-tuple-element.25.own_ref.m_ref), channel_id=1, source_target_pairs={{0,8},{8,0},{16,24},{24,16},{32,40},{40,32},{48,56},{56,48},{64,72... | collective-permute-start | bytes 1867784 | tf_op jit(solution)/shard_map/ppermute | solution.py:19
  33.2 34.3 %copy-start = (f32[1,1024,64]{1,2,0:T(8,128)S(1)}, f32[1,1024,64]{1,2,0:T(8,128)}, u32[]{:S(2)}) copy-start(f32[1,1024,64]{1,2,0:T(8,128)} %param.6) | copy-start | bytes 786436
  33.2 6.6 %collective-permute-start.4 = (bf16[304,1024]{1,0:T(8,128)(2,1)S(1)}, bf16[304,1024]{1,0:T(8,128)(2,1)S(1)}, u32[]{:S(2)}, u32[]{:S(2)}) collective-permute-start(bf16[304,1024]{1,0:T(8,128)(2,1)S(1)} %get-tuple-element.30), channel_id=1, source_target_pairs={{0,8},{8,0},{16,24},{24,16},{32,40},{40,32},{48,56},{56,48},{64,72... | collective-permute-start | bytes 1867784 | tf_op jit(solution)/shard_map/ppermute | solution.py:19
  33.3 15.3 %collective-permute-start.5 = (bf16[304,1024]{1,0:T(8,128)(2,1)S(1)}, bf16[304,1024]{1,0:T(8,128)(2,1)S(1)}, u32[]{:S(2)}, u32[]{:S(2)}) collective-permute-start(bf16[304,1024]{1,0:T(8,128)(2,1)S(1)} %get-tuple-element.31), channel_id=1, source_target_pairs={{8,16},{16,8},{24,32},{32,24},{40,48},{48,40},{56,64},{64,56},{72,... | collective-permute-start | bytes 1867784 | tf_op jit(solution)/shard_map/ppermute | solution.py:19
  51.0 5.1 %collective-permute-start.6 = (bf16[64,1024]{1,0:T(8,128)(2,1)S(1)}, bf16[64,1024]{1,0:T(8,128)(2,1)S(1)}, u32[]{:S(2)}, u32[]{:S(2)}) collective-permute-start(bf16[64,1024]{1,0:T(8,128)(2,1)S(1)} %get-tuple-element.37), channel_id=1, source_target_pairs={{0,4},{1,5},{2,6},{3,7},{4,0},{5,1},{6,2},{7,3},{8,12},{9,13},{10,... | collective-permute-start | bytes 393224 | tf_op jit(solution)/shard_map/ppermute | solution.py:347
  56.1 5.1 %collective-permute-start.7 = (bf16[64,1024]{1,0:T(8,128)(2,1)S(1)}, bf16[64,1024]{1,0:T(8,128)(2,1)S(1)}, u32[]{:S(2)}, u32[]{:S(2)}) collective-permute-start(bf16[64,1024]{1,0:T(8,128)(2,1)S(1)} %add_convert_fusion.1), channel_id=1, source_target_pairs={{0,1},{1,0},{2,3},{3,2},{4,5},{5,4},{6,7},{7,6},{8,9},{9,8},{10,11... | collective-permute-start | bytes 393224 | tf_op jit(solution)/shard_map/ppermute | solution.py:347
  61.2 6.3 %collective-permute-start.8 = (bf16[64,1024]{1,0:T(8,128)(2,1)S(1)}, bf16[64,1024]{1,0:T(8,128)(2,1)S(1)}, u32[]{:S(2)}, u32[]{:S(2)}) collective-permute-start(bf16[64,1024]{1,0:T(8,128)(2,1)S(1)} %add_convert_fusion.v_ref), channel_id=1, source_target_pairs={{0,3},{1,2},{2,1},{3,0},{4,7},{5,6},{6,5},{7,4},{8,11},{9,10},{10,... | collective-permute-start | bytes 393224 | tf_op jit(solution)/shard_map/ppermute | solution.py:347

commit v4 on v3

--- a/solution.py
+++ b/solution.py
@@ -341,15 +341,20 @@
 
     size = lax.axis_size("freq")
     share = points // size
-    value = partial
-    steps = [step for step in (4, 1, 3) if step < size]
-    for step in steps:
-        other = lax.ppermute(value, "freq", [(i, i ^ step) for i in range(size)])
-        if step != steps[-1]:
-            value = (value.astype(F32) + other.astype(F32)).astype(BF)
-
-    def last(c_ref, t_ref, v_ref, o_ref, a_ref, out, g_out, keep):
-        gradient = v_ref[...].astype(F32) + o_ref[...].astype(F32)
+    def partner(value, step):
+        return lax.ppermute(value, "freq", [(i, i ^ step) for i in range(size)])
+
+    value, step = partial, size // 2
+    while step > 2:
+        value = (value.astype(F32) + partner(value, step).astype(F32)).astype(BF)
+        step //= 2
+    others = [partner(value, k) for k in range(1, 2 * step)]
+
+    def last(c_ref, t_ref, a_ref, v_ref, *refs):
+        *o_refs, out, g_out, keep = refs
+        gradient = v_ref[...].astype(F32)
+        for ref in o_refs:
+            gradient = gradient + ref[...].astype(F32)
         keep[...] = gradient
         kernel = ((c_ref[...] - gradient) * t_ref[...].astype(F32)).astype(BF)
         for f in range(nfreq):
@@ -360,7 +365,7 @@
     reflected, mine = call(
         last,
         [shape(nfreq, points, width), shape(count, share, dtype=F32)],
-        [coeffs, table, value, other, angles],
+        [coeffs, table, angles, value, *others],
         near,
         scratch=[pltpu.VMEM((count, points), F32)],
     )

time: 69.1 us -> 67.4 us (0.975)
  waiting for transfers between devices: 24.3 us -> 23.2 us
    ppermute x3 -> x4, waiting for transfers between devices: 9.75 us -> 8.56 us  [partner(): return lax.ppermute(value, 'freq', [(i, i ^ step) for i in range(size)])]
    ppermute x3 -> x4, starting transfers between devices: 4.85 us -> 4.27 us  [partner(): return lax.ppermute(value, 'freq', [(i, i ^ step) for i in range(size)])]
  transfers between devices with their start and end apart: 9 -> 10, of which waited for: 5 -> 5; matrix products, arithmetic and copies ran while one was open for 0% -> 0% of each run, Pallas kernels for 12% -> 13%
where the time goes in v4:
time: 67.4 us; the launch traced here: 67.2 us
  starting transfers between devices  25.6 us (38%)
  waiting for transfers between devices  23.2 us (34%)
  Pallas kernels  17.6 us (26%)
  between operations  0.77 us (1%)
    ppermute x6, starting transfers between devices, exchanged(): return lax.ppermute(block, axis, route)  21.3 us
    pallas_call x8, Pallas kernels, call(): pl.pallas_call(body, out_shape=outs, in_specs=[anywhere if i in hbm else...  17.6 us
    ppermute x6, waiting for transfers between devices, exchanged(): return lax.ppermute(block, axis, route)  14.6 us
    ppermute x4, waiting for transfers between devices, partner(): return lax.ppermute(value, 'freq', [(i, i ^ step) for i in range(size)])  8.56 us
    ppermute x4, starting transfers between devices, partner(): return lax.ppermute(value, 'freq', [(i, i ^ step) for i in range(size)])  4.27 us
  transfers between devices with their start and end apart: 10, of which 5 were waited for; matrix products, arithmetic and copies ran while one was open for 0% of the time, Pallas kernels for 13%

profile of v4, /device:TPU:6, one launch (start us, length us, event | category | flops | bytes accessed | tf_op | source)
XLA Modules:
  0.0 67.2 jit_solution(6369644945559534949)
XLA Ops:
  0.6 1.7 %shard_map.67 = (bf16[96,1024]{1,0:T(8,128)(2,1)S(1)}, bf16[64,1024]{1,0:T(8,128)(2,1)S(1)}) custom-call(bf16[2,1024,256]{2,1,0:T(8,128)(2,1)} %bitcast.14, f32[64,1024]{1,0:T(8,128)} %bitcast.10, bf16[64,1024]{1,0:T(8,128)(2,1)} %constant.2.clone.t_ref), custom_call_target="tpu_custom_call" | custom-call | flops 33554432 | bytes 1441792 | tf_op jit(solution)/shard_map/pallas_call | solution.py:84
  2.3 8.0 %collective-permute-start.1 = (bf16[96,1024]{1,0:T(8,128)(2,1)S(1)}, bf16[96,1024]{1,0:T(8,128)(2,1)S(1)}, u32[]{:S(2)}, u32[]{:S(2)}) collective-permute-start(bf16[96,1024]{1,0:T(8,128)(2,1)S(1)} %get-tuple-element.24.o_ref), channel_id=1, source_target_pairs={{8,16},{16,8},{24,32},{32,24},{40,48},{48,40},{56,64},{64,56},{72,... | collective-permute-start | bytes 589832 | tf_op jit(solution)/shard_map/ppermute | solution.py:19
  10.4 0.1 collective-permute-start
  10.5 4.0 %shard_map.68 = (bf16[2,2,1024,1024]{3,2,1,0:T(8,128)(2,1)S(1)}, bf16[2,128,1024]{2,1,0:T(8,128)(2,1)S(1)}) custom-call(bf16[2,2,1024,1024]{3,2,1,0:T(8,128)(2,1)} %bitcast.12, bf16[64,1024]{1,0:T(8,128)(2,1)S(1)} %get-tuple-element.22.t_ref), custom_call_target="tpu_custom_call" | custom-call | flops 536870912 | bytes 8519680 | tf_op jit(solution)/shard_map/pallas_call | solution.py:84
  14.5 0.0 collective-permute-done.1.far_ref
  14.5 0.0 collective-permute-done.near_ref
  14.5 1.9 %shard_map.69 = (bf16[304,1024]{1,0:T(8,128)(2,1)S(1)}, bf16[2,64,128]{2,1,0:T(8,128)(2,1)S(1)}) custom-call(bf16[2,2,1024,1024]{3,2,1,0:T(8,128)(2,1)S(1)} %get-tuple-element.23.w_ref, bf16[64,1024]{1,0:T(8,128)(2,1)S(1)} %get-tuple-element.22.t_ref, bf16[96,1024]{1,0:T(8,128)(2,1)S(1)} %collective-permute-done.near_ref, ...), custom_call_target="tpu_custom_call" | custom-call | flops 536870912 | bytes 8912896 | tf_op jit(solution)/shard_map/pallas_call | solution.py:84
  16.4 6.5 %collective-permute-start.3 = (bf16[304,1024]{1,0:T(8,128)(2,1)S(1)}, bf16[304,1024]{1,0:T(8,128)(2,1)S(1)}, u32[]{:S(2)}, u32[]{:S(2)}) collective-permute-start(bf16[304,1024]{1,0:T(8,128)(2,1)S(1)} %get-tuple-element.25.own_ref.m_ref), channel_id=1, source_target_pairs={{8,16},{16,8},{24,32},{32,24},{40,48},{48,40},{56,64},{64,56},{72,... | collective-permute-start | bytes 1867784 | tf_op jit(solution)/shard_map/ppermute | solution.py:19
  22.9 0.1 collective-permute-start.2
  23.0 2.7 %shard_map.70 = (bf16[256,1024]{1,0:T(8,128)(2,1)S(1)}, bf16[2,64,128]{2,1,0:T(8,128)(2,1)S(1)}, bf16[2,64,256]{2,1,0:T(8,128)(2,1)S(1)}) custom-call(bf16[2,2,1024,1024]{3,2,1,0:T(8,128)(2,1)S(1)} %get-tuple-element.23.w_ref, bf16[96,1024]{1,0:T(8,128)(2,1)S(1)} %collective-permute-done.near_ref, bf16[96,1024]{1,0:T(8,128)(2,1)S(1)} %collective-permute-done.1.far_ref, ...), custom_call_target="tpu_custom_call" | custom-call | flops 536870912 | bytes 9961472 | tf_op jit(solution)/shard_map/pallas_call | solution.py:84
  25.8 5.8 %collective-permute-done.3.far_ref = bf16[304,1024]{1,0:T(8,128)(2,1)S(1)} collective-permute-done((bf16[304,1024]{1,0:T(8,128)(2,1)S(1)}, bf16[304,1024]{1,0:T(8,128)(2,1)S(1)}, u32[]{:S(2)}, u32[]{:S(2)}) %collective-permute-start.3) | collective-permute-done | bytes 622624 | tf_op jit(solution)/shard_map/ppermute | solution.py:19
  31.6 0.0 collective-permute-done.2.near_ref
  31.6 1.6 %shard_map.71 = (bf16[288,1024]{1,0:T(8,128)(2,1)S(1)}, bf16[304,1024]{1,0:T(8,128)(2,1)S(1)}, bf16[304,1024]{1,0:T(8,128)(2,1)S(1)}, bf16[2,64,256]{2,1,0:T(8,128)(2,1)S(1)}) custom-call(bf16[2,2,1024,1024]{3,2,1,0:T(8,128)(2,1)S(1)} %get-tuple-element.23.w_ref, bf16[64,1024]{1,0:T(8,128)(2,1)S(1)} %get-tuple-element.22.t_ref, ...), custom_call_target="tpu_custom_call" | custom-call | flops 1073741824 | bytes 10518528 | tf_op jit(solution)/shard_map/pallas_call | solution.py:84
  33.2 0.0 copy-start
  33.2 0.1 collective-permute-start.4
  33.3 6.5 %collective-permute-start.5 = (bf16[304,1024]{1,0:T(8,128)(2,1)S(1)}, bf16[304,1024]{1,0:T(8,128)(2,1)S(1)}, u32[]{:S(2)}, u32[]{:S(2)}) collective-permute-start(bf16[304,1024]{1,0:T(8,128)(2,1)S(1)} %get-tuple-element.31), channel_id=1, source_target_pairs={{8,16},{16,8},{24,32},{32,24},{40,48},{48,40},{56,64},{64,56},{72,... | collective-permute-start | bytes 1867784 | tf_op jit(solution)/shard_map/ppermute | solution.py:19
  39.8 0.0 collective-permute-done.4.near_ref
  39.8 8.8 %collective-permute-done.5.far_ref = bf16[304,1024]{1,0:T(8,128)(2,1)S(1)} collective-permute-done((bf16[304,1024]{1,0:T(8,128)(2,1)S(1)}, bf16[304,1024]{1,0:T(8,128)(2,1)S(1)}, u32[]{:S(2)}, u32[]{:S(2)}) %collective-permute-start.5) | collective-permute-done | bytes 622624 | tf_op jit(solution)/shard_map/ppermute | solution.py:19
  48.6 2.4 %shard_map.72 = (bf16[2,128,1024]{2,1,0:T(8,128)(2,1)S(1)}, bf16[2,384,256]{2,1,0:T(8,128)(2,1)S(1)}, bf16[64,1024]{1,0:T(8,128)(2,1)S(1)}, bf16[2,64,256]{2,1,0:T(8,128)(2,1)S(1)}) custom-call(bf16[2,2,1024,1024]{3,2,1,0:T(8,128)(2,1)S(1)} %get-tuple-element.23.w_ref, bf16[304,1024]{1,0:T(8,128)(2,1)S(1)} %collective-permute-done.4.near_ref, ...), custom_call_target="tpu_custom_call" | custom-call | flops 1241513984 | bytes 11730944 | tf_op jit(solution)/shard_map/pallas_call | solution.py:84
  51.0 0.1 collective-permute-start.6
  51.1 5.0 %collective-permute-done.6 = bf16[64,1024]{1,0:T(8,128)(2,1)S(1)} collective-permute-done((bf16[64,1024]{1,0:T(8,128)(2,1)S(1)}, bf16[64,1024]{1,0:T(8,128)(2,1)S(1)}, u32[]{:S(2)}, u32[]{:S(2)}) %collective-permute-start.6) | collective-permute-done | bytes 131104 | tf_op jit(solution)/shard_map/ppermute | solution.py:345
  56.1 3.1 %collective-permute-start.9 = (bf16[64,1024]{1,0:T(8,128)(2,1)S(1)}, bf16[64,1024]{1,0:T(8,128)(2,1)S(1)}, u32[]{:S(2)}, u32[]{:S(2)}) collective-permute-start(bf16[64,1024]{1,0:T(8,128)(2,1)S(1)} %add_convert_fusion.v_ref), channel_id=1, source_target_pairs={{0,3},{1,2},{2,1},{3,0},{4,7},{5,6},{6,5},{7,4},{8,11},{9,10},{10,... | collective-permute-start | bytes 393224 | tf_op jit(solution)/shard_map/ppermute | solution.py:345
  59.2 0.6 collective-permute-start.8
  59.9 0.5 collective-permute-start.7
  60.3 1.8 %shard_map.73 = bf16[2,1024,256]{2,1,0:T(8,128)(2,1)} custom-call(bf16[2,128,1024]{2,1,0:T(8,128)(2,1)S(1)} %get-tuple-element.35.q_ref, bf16[288,1024]{1,0:T(8,128)(2,1)S(1)} %get-tuple-element.32.n_ref, bf16[304,1024]{1,0:T(8,128)(2,1)S(1)} %get-tuple-element.25.own_ref.m_ref, bf16[2,384,256]{2,1,0:T(8,128)(2,1)S(1)} %get-tuple-element.36.f_ref), custom_call_target="tpu_custom_call" | custom-call | flops 100663296 | bytes 2129920 | tf_op jit(solution)/shard_map/pallas_call | solution.py:84
  62.1 1.1 %collective-permute-done.9.refs_2_ = bf16[64,1024]{1,0:T(8,128)(2,1)S(1)} collective-permute-done((bf16[64,1024]{1,0:T(8,128)(2,1)S(1)}, bf16[64,1024]{1,0:T(8,128)(2,1)S(1)}, u32[]{:S(2)}, u32[]{:S(2)}) %collective-permute-start.9) | collective-permute-done | bytes 131104 | tf_op jit(solution)/shard_map/ppermute | solution.py:345
  63.2 2.5 %collective-permute-done.8.refs_1_ = bf16[64,1024]{1,0:T(8,128)(2,1)S(1)} collective-permute-done((bf16[64,1024]{1,0:T(8,128)(2,1)S(1)}, bf16[64,1024]{1,0:T(8,128)(2,1)S(1)}, u32[]{:S(2)}, u32[]{:S(2)}) %collective-permute-start.8) | collective-permute-done | bytes 131104 | tf_op jit(solution)/shard_map/ppermute | solution.py:345
  65.7 0.0 collective-permute-done.7.refs_0_
  65.7 0.0 copy-done
  65.7 1.5 %shard_map.74 = (bf16[2,1024,256]{2,1,0:T(8,128)(2,1)}, f32[64,128]{1,0:T(8,128)}) custom-call(f32[64,1024]{1,0:T(8,128)S(1)} %bitcast.11, bf16[64,1024]{1,0:T(8,128)(2,1)S(1)} %get-tuple-element.22.t_ref, bf16[2,64,256]{2,1,0:T(8,128)(2,1)S(1)} %get-tuple-element.37.a_ref, bf16[64,1024]{1,0:T(8,128)(2,1)S(1)} %add_convert_fusion.v_ref, ...), custom_call_target="tpu_custom_call" | custom-call | flops 33554432 | bytes 983040 | tf_op jit(solution)/shard_map/pallas_call | solution.py:84
  (1 shorter events, 0.0 us)
Async XLA Ops:
  2.3 12.2 %collective-permute-start.1 = (bf16[96,1024]{1,0:T(8,128)(2,1)S(1)}, bf16[96,1024]{1,0:T(8,128)(2,1)S(1)}, u32[]{:S(2)}, u32[]{:S(2)}) collective-permute-start(bf16[96,1024]{1,0:T(8,128)(2,1)S(1)} %get-tuple-element.24.o_ref), channel_id=1, source_target_pairs={{8,16},{16,8},{24,32},{32,24},{40,48},{48,40},{56,64},{64,56},{72,... | collective-permute-start | bytes 589832 | tf_op jit(solution)/shard_map/ppermute | solution.py:19
  10.4 4.1 %collective-permute-start = (bf16[96,1024]{1,0:T(8,128)(2,1)S(1)}, bf16[96,1024]{1,0:T(8,128)(2,1)S(1)}, u32[]{:S(2)}, u32[]{:S(2)}) collective-permute-start(bf16[96,1024]{1,0:T(8,128)(2,1)S(1)} %get-tuple-element.24.o_ref), channel_id=1, source_target_pairs={{0,8},{8,0},{16,24},{24,16},{32,40},{40,32},{48,56},{56,48},{64,72... | collective-permute-start | bytes 589832 | tf_op jit(solution)/shard_map/ppermute | solution.py:19
  16.4 15.2 %collective-permute-start.3 = (bf16[304,1024]{1,0:T(8,128)(2,1)S(1)}, bf16[304,1024]{1,0:T(8,128)(2,1)S(1)}, u32[]{:S(2)}, u32[]{:S(2)}) collective-permute-start(bf16[304,1024]{1,0:T(8,128)(2,1)S(1)} %get-tuple-element.25.own_ref.m_ref), channel_id=1, source_target_pairs={{8,16},{16,8},{24,32},{32,24},{40,48},{48,40},{56,64},{64,56},{72,... | collective-permute-start | bytes 1867784 | tf_op jit(solution)/shard_map/ppermute | solution.py:19
  22.9 8.7 %collective-permute-start.2 = (bf16[304,1024]{1,0:T(8,128)(2,1)S(1)}, bf16[304,1024]{1,0:T(8,128)(2,1)S(1)}, u32[]{:S(2)}, u32[]{:S(2)}) collective-permute-start(bf16[304,1024]{1,0:T(8,128)(2,1)S(1)} %get-tuple-element.25.own_ref.m_ref), channel_id=1, source_target_pairs={{0,8},{8,0},{16,24},{24,16},{32,40},{40,32},{48,56},{56,48},{64,72... | collective-permute-start | bytes 1867784 | tf_op jit(solution)/shard_map/ppermute | solution.py:19
  33.2 32.5 %copy-start = (f32[1,1024,64]{1,2,0:T(8,128)S(1)}, f32[1,1024,64]{1,2,0:T(8,128)}, u32[]{:S(2)}) copy-start(f32[1,1024,64]{1,2,0:T(8,128)} %param.6) | copy-start | bytes 786436
  33.2 6.6 %collective-permute-start.4 = (bf16[304,1024]{1,0:T(8,128)(2,1)S(1)}, bf16[304,1024]{1,0:T(8,128)(2,1)S(1)}, u32[]{:S(2)}, u32[]{:S(2)}) collective-permute-start(bf16[304,1024]{1,0:T(8,128)(2,1)S(1)} %get-tuple-element.30), channel_id=1, source_target_pairs={{0,8},{8,0},{16,24},{24,16},{32,40},{40,32},{48,56},{56,48},{64,72... | collective-permute-start | bytes 1867784 | tf_op jit(solution)/shard_map/ppermute | solution.py:19
  33.3 15.3 %collective-permute-start.5 = (bf16[304,1024]{1,0:T(8,128)(2,1)S(1)}, bf16[304,1024]{1,0:T(8,128)(2,1)S(1)}, u32[]{:S(2)}, u32[]{:S(2)}) collective-permute-start(bf16[304,1024]{1,0:T(8,128)(2,1)S(1)} %get-tuple-element.31), channel_id=1, source_target_pairs={{8,16},{16,8},{24,32},{32,24},{40,48},{48,40},{56,64},{64,56},{72,... | collective-permute-start | bytes 1867784 | tf_op jit(solution)/shard_map/ppermute | solution.py:19
  51.0 5.1 %collective-permute-start.6 = (bf16[64,1024]{1,0:T(8,128)(2,1)S(1)}, bf16[64,1024]{1,0:T(8,128)(2,1)S(1)}, u32[]{:S(2)}, u32[]{:S(2)}) collective-permute-start(bf16[64,1024]{1,0:T(8,128)(2,1)S(1)} %get-tuple-element.38), channel_id=1, source_target_pairs={{0,4},{1,5},{2,6},{3,7},{4,0},{5,1},{6,2},{7,3},{8,12},{9,13},{10,... | collective-permute-start | bytes 393224 | tf_op jit(solution)/shard_map/ppermute | solution.py:345
  56.1 7.0 %collective-permute-start.9 = (bf16[64,1024]{1,0:T(8,128)(2,1)S(1)}, bf16[64,1024]{1,0:T(8,128)(2,1)S(1)}, u32[]{:S(2)}, u32[]{:S(2)}) collective-permute-start(bf16[64,1024]{1,0:T(8,128)(2,1)S(1)} %add_convert_fusion.v_ref), channel_id=1, source_target_pairs={{0,3},{1,2},{2,1},{3,0},{4,7},{5,6},{6,5},{7,4},{8,11},{9,10},{10,... | collective-permute-start | bytes 393224 | tf_op jit(solution)/shard_map/ppermute | solution.py:345
  59.2 6.5 %collective-permute-start.8 = (bf16[64,1024]{1,0:T(8,128)(2,1)S(1)}, bf16[64,1024]{1,0:T(8,128)(2,1)S(1)}, u32[]{:S(2)}, u32[]{:S(2)}) collective-permute-start(bf16[64,1024]{1,0:T(8,128)(2,1)S(1)} %add_convert_fusion.v_ref), channel_id=1, source_target_pairs={{0,2},{1,3},{2,0},{3,1},{4,6},{5,7},{6,4},{7,5},{8,10},{9,11},{10,... | collective-permute-start | bytes 393224 | tf_op jit(solution)/shard_map/ppermute | solution.py:345
  59.9 5.9 %collective-permute-start.7 = (bf16[64,1024]{1,0:T(8,128)(2,1)S(1)}, bf16[64,1024]{1,0:T(8,128)(2,1)S(1)}, u32[]{:S(2)}, u32[]{:S(2)}) collective-permute-start(bf16[64,1024]{1,0:T(8,128)(2,1)S(1)} %add_convert_fusion.v_ref), channel_id=1, source_target_pairs={{0,1},{1,0},{2,3},{3,2},{4,5},{5,4},{6,7},{7,6},{8,9},{9,8},{10,11... | collective-permute-start | bytes 393224 | tf_op jit(solution)/shard_map/ppermute | solution.py:345

commit v5 on v4

--- a/solution.py
+++ b/solution.py
@@ -270,13 +270,36 @@
     )
     near3, far3 = swap(x3, y3)
 
+    def make_q_near(w_ref, near_ref, out):
+        @pl.when(is_even("depth"))
+        def _():
+            for f in range(nfreq):
+                out[f] = advance(w_ref, near_ref[f * panel : (f + 1) * panel], f)
+
+        @pl.when(jnp.logical_not(is_even("depth")))
+        def _():
+            out[...] = jnp.zeros(out.shape, BF)
+
+    (q_near,) = call(
+        make_q_near, [shape(nfreq, panel, points)], [kept, near3], whole
+    )
+
     scale = float(1.0 / np.sqrt(np.float32(width // 2 * nfreq * lax.axis_size("freq"))))
 
     def make_q(
-        w_ref, near_ref, far_ref, n_ref, m_ref, s_ref, g_ref, o_ref, u_ref, v_ref,
+        w_ref, near_ref, far_ref, n_ref, m_ref, s_ref, g_ref, o_ref, u_ref, v_ref, q_ref,
         q_out, f_out, c_out, a_out
     ):
         partial = jnp.zeros((count, points), F32)
+        @pl.when(is_even("depth"))
+        def _():
+            q_out[...] = q_ref[...]
+
+        @pl.when(jnp.logical_not(is_even("depth")))
+        def _():
+            for f in range(nfreq):
+                q_out[f] = advance(w_ref, far_ref[f * panel : (f + 1) * panel], f)
+
         tail = from_below(near_ref, far_ref, body, height)
         above = from_above(near_ref, far_ref, body, height)
         for f in range(nfreq):
@@ -294,9 +317,7 @@
             angles = (start.astype(F32) - down3).astype(BF)
             a_out[f] = angles
 
-            n = from_below(near_ref, far_ref, f * panel, (f + 1) * panel)
-            q = advance(w_ref, n, f)
-            q_out[f] = q
+            q = q_out[f]
             start2 = unpack(n_ref, low, 0, count, width)
             start3 = unpack(tail, f * rows, 0, count, width)
             turn = unpack(tail, total, f * spread, count, panel)
@@ -319,7 +340,7 @@
             shape(count, points),
             shape(nfreq, count, width),
         ],
-        [kept, near3, far3, own3, own2, seen, g, own1, tu1, tu1_above],
+        [kept, near3, far3, own3, own2, seen, g, own1, tu1, tu1_above, q_near],
         whole + 5 * near,
     )
 
@@ -348,7 +369,7 @@
     while step > 2:
         value = (value.astype(F32) + partner(value, step).astype(F32)).astype(BF)
         step //= 2
-    others = [partner(value, k) for k in range(1, 2 * step)]
+    others = [partner(value, k) for k in (1, 3, 2)[: 2 * step - 1]]
 
     def last(c_ref, t_ref, a_ref, v_ref, *refs):
         *o_refs, out, g_out, keep = refs

time: 67.4 us -> 66.3 us (0.984)
  waiting for transfers between devices: 23.2 us -> 21.6 us
    ppermute x6, waiting for transfers between devices: 14.6 us -> 13.3 us  [exchanged(): return lax.ppermute(block, axis, route)]
    pallas_call x8 -> x9, Pallas kernels: 17.6 us -> 18 us  [call(): pl.pallas_call(body, out_shape=outs, in_specs=[anywhere if i in hbm else...]
  transfers between devices with their start and end apart: 10 -> 10, of which waited for: 5 -> 5; matrix products, arithmetic and copies ran while one was open for 0% -> 0% of each run, Pallas kernels for 13% -> 15%
where the time goes in v5:
time: 66.3 us; the launch traced here: 66.1 us
  starting transfers between devices  25.7 us (39%)
  waiting for transfers between devices  21.6 us (33%)
  Pallas kernels  18 us (27%)
  between operations  0.78 us (1%)
    ppermute x6, starting transfers between devices, exchanged(): return lax.ppermute(block, axis, route)  21.3 us
    pallas_call x9, Pallas kernels, call(): pl.pallas_call(body, out_shape=outs, in_specs=[anywhere if i in hbm else...  18 us
    ppermute x6, waiting for transfers between devices, exchanged(): return lax.ppermute(block, axis, route)  13.3 us
    ppermute x4, waiting for transfers between devices, partner(): return lax.ppermute(value, 'freq', [(i, i ^ step) for i in range(size)])  8.32 us
    ppermute x4, starting transfers between devices, partner(): return lax.ppermute(value, 'freq', [(i, i ^ step) for i in range(size)])  4.42 us
  transfers between devices with their start and end apart: 10, of which 5 were waited for; matrix products, arithmetic and copies ran while one was open for 0% of the time, Pallas kernels for 15%

profile of v5, /device:TPU:6, one launch (start us, length us, event | category | flops | bytes accessed | tf_op | source)
XLA Modules:
  0.0 66.1 jit_solution(14453878677138530758)
XLA Ops:
  0.6 1.7 %shard_map.67 = (bf16[96,1024]{1,0:T(8,128)(2,1)S(1)}, bf16[64,1024]{1,0:T(8,128)(2,1)S(1)}) custom-call(bf16[2,1024,256]{2,1,0:T(8,128)(2,1)} %bitcast.14, f32[64,1024]{1,0:T(8,128)} %bitcast.10, bf16[64,1024]{1,0:T(8,128)(2,1)} %constant.2.clone.t_ref), custom_call_target="tpu_custom_call" | custom-call | flops 33554432 | bytes 1441792 | tf_op jit(solution)/shard_map/pallas_call | solution.py:84
  2.3 8.0 %collective-permute-start.1 = (bf16[96,1024]{1,0:T(8,128)(2,1)S(1)}, bf16[96,1024]{1,0:T(8,128)(2,1)S(1)}, u32[]{:S(2)}, u32[]{:S(2)}) collective-permute-start(bf16[96,1024]{1,0:T(8,128)(2,1)S(1)} %get-tuple-element.24.o_ref), channel_id=1, source_target_pairs={{8,16},{16,8},{24,32},{32,24},{40,48},{48,40},{56,64},{64,56},{72,... | collective-permute-start | bytes 589832 | tf_op jit(solution)/shard_map/ppermute | solution.py:19
  10.4 0.1 collective-permute-start
  10.5 4.0 %shard_map.68 = (bf16[2,2,1024,1024]{3,2,1,0:T(8,128)(2,1)S(1)}, bf16[2,128,1024]{2,1,0:T(8,128)(2,1)S(1)}) custom-call(bf16[2,2,1024,1024]{3,2,1,0:T(8,128)(2,1)} %bitcast.12, bf16[64,1024]{1,0:T(8,128)(2,1)S(1)} %get-tuple-element.22.t_ref), custom_call_target="tpu_custom_call" | custom-call | flops 536870912 | bytes 8519680 | tf_op jit(solution)/shard_map/pallas_call | solution.py:84
  14.5 0.0 collective-permute-done.1.far_ref
  14.5 0.0 collective-permute-done.near_ref
  14.5 1.9 %shard_map.69 = (bf16[304,1024]{1,0:T(8,128)(2,1)S(1)}, bf16[2,64,128]{2,1,0:T(8,128)(2,1)S(1)}) custom-call(bf16[2,2,1024,1024]{3,2,1,0:T(8,128)(2,1)S(1)} %get-tuple-element.23.w_ref, bf16[64,1024]{1,0:T(8,128)(2,1)S(1)} %get-tuple-element.22.t_ref, bf16[96,1024]{1,0:T(8,128)(2,1)S(1)} %collective-permute-done.near_ref, ...), custom_call_target="tpu_custom_call" | custom-call | flops 536870912 | bytes 8912896 | tf_op jit(solution)/shard_map/pallas_call | solution.py:84
  16.4 6.5 %collective-permute-start.3 = (bf16[304,1024]{1,0:T(8,128)(2,1)S(1)}, bf16[304,1024]{1,0:T(8,128)(2,1)S(1)}, u32[]{:S(2)}, u32[]{:S(2)}) collective-permute-start(bf16[304,1024]{1,0:T(8,128)(2,1)S(1)} %get-tuple-element.25.own_ref.m_ref), channel_id=1, source_target_pairs={{8,16},{16,8},{24,32},{32,24},{40,48},{48,40},{56,64},{64,56},{72,... | collective-permute-start | bytes 1867784 | tf_op jit(solution)/shard_map/ppermute | solution.py:19
  22.9 0.1 collective-permute-start.2
  23.0 2.7 %shard_map.70 = (bf16[256,1024]{1,0:T(8,128)(2,1)S(1)}, bf16[2,64,128]{2,1,0:T(8,128)(2,1)S(1)}, bf16[2,64,256]{2,1,0:T(8,128)(2,1)S(1)}) custom-call(bf16[2,2,1024,1024]{3,2,1,0:T(8,128)(2,1)S(1)} %get-tuple-element.23.w_ref, bf16[96,1024]{1,0:T(8,128)(2,1)S(1)} %collective-permute-done.near_ref, bf16[96,1024]{1,0:T(8,128)(2,1)S(1)} %collective-permute-done.1.far_ref, ...), custom_call_target="tpu_custom_call" | custom-call | flops 536870912 | bytes 9961472 | tf_op jit(solution)/shard_map/pallas_call | solution.py:84
  25.8 5.8 %collective-permute-done.3.far_ref = bf16[304,1024]{1,0:T(8,128)(2,1)S(1)} collective-permute-done((bf16[304,1024]{1,0:T(8,128)(2,1)S(1)}, bf16[304,1024]{1,0:T(8,128)(2,1)S(1)}, u32[]{:S(2)}, u32[]{:S(2)}) %collective-permute-start.3) | collective-permute-done | bytes 622624 | tf_op jit(solution)/shard_map/ppermute | solution.py:19
  31.6 0.0 collective-permute-done.2.near_ref
  31.6 1.6 %shard_map.71 = (bf16[288,1024]{1,0:T(8,128)(2,1)S(1)}, bf16[304,1024]{1,0:T(8,128)(2,1)S(1)}, bf16[304,1024]{1,0:T(8,128)(2,1)S(1)}, bf16[2,64,256]{2,1,0:T(8,128)(2,1)S(1)}) custom-call(bf16[2,2,1024,1024]{3,2,1,0:T(8,128)(2,1)S(1)} %get-tuple-element.23.w_ref, bf16[64,1024]{1,0:T(8,128)(2,1)S(1)} %get-tuple-element.22.t_ref, ...), custom_call_target="tpu_custom_call" | custom-call | flops 1073741824 | bytes 10518528 | tf_op jit(solution)/shard_map/pallas_call | solution.py:84
  33.2 0.1 collective-permute-start.4
  33.3 6.5 %collective-permute-start.5 = (bf16[304,1024]{1,0:T(8,128)(2,1)S(1)}, bf16[304,1024]{1,0:T(8,128)(2,1)S(1)}, u32[]{:S(2)}, u32[]{:S(2)}) collective-permute-start(bf16[304,1024]{1,0:T(8,128)(2,1)S(1)} %get-tuple-element.31), channel_id=1, source_target_pairs={{8,16},{16,8},{24,32},{32,24},{40,48},{48,40},{56,64},{64,56},{72,... | collective-permute-start | bytes 1867784 | tf_op jit(solution)/shard_map/ppermute | solution.py:19
  39.8 0.0 collective-permute-done.4.near_ref
  39.8 1.3 %shard_map.72.q_ref = bf16[2,128,1024]{2,1,0:T(8,128)(2,1)S(1)} custom-call(bf16[2,2,1024,1024]{3,2,1,0:T(8,128)(2,1)S(1)} %get-tuple-element.23.w_ref, bf16[304,1024]{1,0:T(8,128)(2,1)S(1)} %collective-permute-done.4.near_ref), custom_call_target="tpu_custom_call" | custom-call | flops 1073741824 | bytes 9011200 | tf_op jit(solution)/shard_map/pallas_call | solution.py:84
  41.1 0.0 copy-start
  41.1 7.5 %collective-permute-done.5.far_ref = bf16[304,1024]{1,0:T(8,128)(2,1)S(1)} collective-permute-done((bf16[304,1024]{1,0:T(8,128)(2,1)S(1)}, bf16[304,1024]{1,0:T(8,128)(2,1)S(1)}, u32[]{:S(2)}, u32[]{:S(2)}) %collective-permute-start.5) | collective-permute-done | bytes 622624 | tf_op jit(solution)/shard_map/ppermute | solution.py:19
  48.6 1.5 %shard_map.73 = (bf16[2,128,1024]{2,1,0:T(8,128)(2,1)S(1)}, bf16[2,384,256]{2,1,0:T(8,128)(2,1)S(1)}, bf16[64,1024]{1,0:T(8,128)(2,1)S(1)}, bf16[2,64,256]{2,1,0:T(8,128)(2,1)S(1)}) custom-call(bf16[2,2,1024,1024]{3,2,1,0:T(8,128)(2,1)S(1)} %get-tuple-element.23.w_ref, bf16[304,1024]{1,0:T(8,128)(2,1)S(1)} %collective-permute-done.4.near_ref, ...), custom_call_target="tpu_custom_call" | custom-call | flops 1241513984 | bytes 12255232 | tf_op jit(solution)/shard_map/pallas_call | solution.py:84
  50.1 0.1 collective-permute-start.6
  50.2 5.0 %collective-permute-done.6 = bf16[64,1024]{1,0:T(8,128)(2,1)S(1)} collective-permute-done((bf16[64,1024]{1,0:T(8,128)(2,1)S(1)}, bf16[64,1024]{1,0:T(8,128)(2,1)S(1)}, u32[]{:S(2)}, u32[]{:S(2)}) %collective-permute-start.6) | collective-permute-done | bytes 131104 | tf_op jit(solution)/shard_map/ppermute | solution.py:366
  55.2 3.3 %collective-permute-start.9 = (bf16[64,1024]{1,0:T(8,128)(2,1)S(1)}, bf16[64,1024]{1,0:T(8,128)(2,1)S(1)}, u32[]{:S(2)}, u32[]{:S(2)}) collective-permute-start(bf16[64,1024]{1,0:T(8,128)(2,1)S(1)} %add_convert_fusion.v_ref), channel_id=1, source_target_pairs={{0,2},{1,3},{2,0},{3,1},{4,6},{5,7},{6,4},{7,5},{8,10},{9,11},{10,... | collective-permute-start | bytes 393224 | tf_op jit(solution)/shard_map/ppermute | solution.py:366
  58.5 1.0 %collective-permute-start.8 = (bf16[64,1024]{1,0:T(8,128)(2,1)S(1)}, bf16[64,1024]{1,0:T(8,128)(2,1)S(1)}, u32[]{:S(2)}, u32[]{:S(2)}) collective-permute-start(bf16[64,1024]{1,0:T(8,128)(2,1)S(1)} %add_convert_fusion.v_ref), channel_id=1, source_target_pairs={{0,3},{1,2},{2,1},{3,0},{4,7},{5,6},{6,5},{7,4},{8,11},{9,10},{10,... | collective-permute-start | bytes 393224 | tf_op jit(solution)/shard_map/ppermute | solution.py:366
  59.5 0.0 collective-permute-start.7
  59.5 1.8 %shard_map.74 = bf16[2,1024,256]{2,1,0:T(8,128)(2,1)} custom-call(bf16[2,128,1024]{2,1,0:T(8,128)(2,1)S(1)} %get-tuple-element.35.q_ref, bf16[288,1024]{1,0:T(8,128)(2,1)S(1)} %get-tuple-element.32.n_ref, bf16[304,1024]{1,0:T(8,128)(2,1)S(1)} %get-tuple-element.25.own_ref.m_ref, bf16[2,384,256]{2,1,0:T(8,128)(2,1)S(1)} %get-tuple-element.36.f_ref), custom_call_target="tpu_custom_call" | custom-call | flops 100663296 | bytes 2129920 | tf_op jit(solution)/shard_map/pallas_call | solution.py:84
  61.3 1.8 %collective-permute-done.9.refs_2_ = bf16[64,1024]{1,0:T(8,128)(2,1)S(1)} collective-permute-done((bf16[64,1024]{1,0:T(8,128)(2,1)S(1)}, bf16[64,1024]{1,0:T(8,128)(2,1)S(1)}, u32[]{:S(2)}, u32[]{:S(2)}) %collective-permute-start.9) | collective-permute-done | bytes 131104 | tf_op jit(solution)/shard_map/ppermute | solution.py:366
  63.1 1.5 %collective-permute-done.8.refs_1_ = bf16[64,1024]{1,0:T(8,128)(2,1)S(1)} collective-permute-done((bf16[64,1024]{1,0:T(8,128)(2,1)S(1)}, bf16[64,1024]{1,0:T(8,128)(2,1)S(1)}, u32[]{:S(2)}, u32[]{:S(2)}) %collective-permute-start.8) | collective-permute-done | bytes 131104 | tf_op jit(solution)/shard_map/ppermute | solution.py:366
  64.7 0.0 collective-permute-done.7.refs_0_
  64.7 0.0 copy-done
  64.7 1.5 %shard_map.75 = (bf16[2,1024,256]{2,1,0:T(8,128)(2,1)}, f32[64,128]{1,0:T(8,128)}) custom-call(f32[64,1024]{1,0:T(8,128)S(1)} %bitcast.11, bf16[64,1024]{1,0:T(8,128)(2,1)S(1)} %get-tuple-element.22.t_ref, bf16[2,64,256]{2,1,0:T(8,128)(2,1)S(1)} %get-tuple-element.37.a_ref, bf16[64,1024]{1,0:T(8,128)(2,1)S(1)} %add_convert_fusion.v_ref, ...), custom_call_target="tpu_custom_call" | custom-call | flops 33554432 | bytes 983040 | tf_op jit(solution)/shard_map/pallas_call | solution.py:84
  (1 shorter events, 0.0 us)
Async XLA Ops:
  2.3 12.2 %collective-permute-start.1 = (bf16[96,1024]{1,0:T(8,128)(2,1)S(1)}, bf16[96,1024]{1,0:T(8,128)(2,1)S(1)}, u32[]{:S(2)}, u32[]{:S(2)}) collective-permute-start(bf16[96,1024]{1,0:T(8,128)(2,1)S(1)} %get-tuple-element.24.o_ref), channel_id=1, source_target_pairs={{8,16},{16,8},{24,32},{32,24},{40,48},{48,40},{56,64},{64,56},{72,... | collective-permute-start | bytes 589832 | tf_op jit(solution)/shard_map/ppermute | solution.py:19
  10.4 4.1 %collective-permute-start = (bf16[96,1024]{1,0:T(8,128)(2,1)S(1)}, bf16[96,1024]{1,0:T(8,128)(2,1)S(1)}, u32[]{:S(2)}, u32[]{:S(2)}) collective-permute-start(bf16[96,1024]{1,0:T(8,128)(2,1)S(1)} %get-tuple-element.24.o_ref), channel_id=1, source_target_pairs={{0,8},{8,0},{16,24},{24,16},{32,40},{40,32},{48,56},{56,48},{64,72... | collective-permute-start | bytes 589832 | tf_op jit(solution)/shard_map/ppermute | solution.py:19
  16.4 15.2 %collective-permute-start.3 = (bf16[304,1024]{1,0:T(8,128)(2,1)S(1)}, bf16[304,1024]{1,0:T(8,128)(2,1)S(1)}, u32[]{:S(2)}, u32[]{:S(2)}) collective-permute-start(bf16[304,1024]{1,0:T(8,128)(2,1)S(1)} %get-tuple-element.25.own_ref.m_ref), channel_id=1, source_target_pairs={{8,16},{16,8},{24,32},{32,24},{40,48},{48,40},{56,64},{64,56},{72,... | collective-permute-start | bytes 1867784 | tf_op jit(solution)/shard_map/ppermute | solution.py:19
  22.9 8.7 %collective-permute-start.2 = (bf16[304,1024]{1,0:T(8,128)(2,1)S(1)}, bf16[304,1024]{1,0:T(8,128)(2,1)S(1)}, u32[]{:S(2)}, u32[]{:S(2)}) collective-permute-start(bf16[304,1024]{1,0:T(8,128)(2,1)S(1)} %get-tuple-element.25.own_ref.m_ref), channel_id=1, source_target_pairs={{0,8},{8,0},{16,24},{24,16},{32,40},{40,32},{48,56},{56,48},{64,72... | collective-permute-start | bytes 1867784 | tf_op jit(solution)/shard_map/ppermute | solution.py:19
  33.2 6.6 %collective-permute-start.4 = (bf16[304,1024]{1,0:T(8,128)(2,1)S(1)}, bf16[304,1024]{1,0:T(8,128)(2,1)S(1)}, u32[]{:S(2)}, u32[]{:S(2)}) collective-permute-start(bf16[304,1024]{1,0:T(8,128)(2,1)S(1)} %get-tuple-element.30), channel_id=1, source_target_pairs={{0,8},{8,0},{16,24},{24,16},{32,40},{40,32},{48,56},{56,48},{64,72... | collective-permute-start | bytes 1867784 | tf_op jit(solution)/shard_map/ppermute | solution.py:19
  33.3 15.3 %collective-permute-start.5 = (bf16[304,1024]{1,0:T(8,128)(2,1)S(1)}, bf16[304,1024]{1,0:T(8,128)(2,1)S(1)}, u32[]{:S(2)}, u32[]{:S(2)}) collective-permute-start(bf16[304,1024]{1,0:T(8,128)(2,1)S(1)} %get-tuple-element.31), channel_id=1, source_target_pairs={{8,16},{16,8},{24,32},{32,24},{40,48},{48,40},{56,64},{64,56},{72,... | collective-permute-start | bytes 1867784 | tf_op jit(solution)/shard_map/ppermute | solution.py:19
  41.1 23.6 %copy-start = (f32[1,1024,64]{1,2,0:T(8,128)S(1)}, f32[1,1024,64]{1,2,0:T(8,128)}, u32[]{:S(2)}) copy-start(f32[1,1024,64]{1,2,0:T(8,128)} %param.6) | copy-start | bytes 786436
  50.1 5.1 %collective-permute-start.6 = (bf16[64,1024]{1,0:T(8,128)(2,1)S(1)}, bf16[64,1024]{1,0:T(8,128)(2,1)S(1)}, u32[]{:S(2)}, u32[]{:S(2)}) collective-permute-start(bf16[64,1024]{1,0:T(8,128)(2,1)S(1)} %get-tuple-element.38), channel_id=1, source_target_pairs={{0,4},{1,5},{2,6},{3,7},{4,0},{5,1},{6,2},{7,3},{8,12},{9,13},{10,... | collective-permute-start | bytes 393224 | tf_op jit(solution)/shard_map/ppermute | solution.py:366
  55.2 7.9 %collective-permute-start.9 = (bf16[64,1024]{1,0:T(8,128)(2,1)S(1)}, bf16[64,1024]{1,0:T(8,128)(2,1)S(1)}, u32[]{:S(2)}, u32[]{:S(2)}) collective-permute-start(bf16[64,1024]{1,0:T(8,128)(2,1)S(1)} %add_convert_fusion.v_ref), channel_id=1, source_target_pairs={{0,2},{1,3},{2,0},{3,1},{4,6},{5,7},{6,4},{7,5},{8,10},{9,11},{10,... | collective-permute-start | bytes 393224 | tf_op jit(solution)/shard_map/ppermute | solution.py:366
  58.5 6.2 %collective-permute-start.8 = (bf16[64,1024]{1,0:T(8,128)(2,1)S(1)}, bf16[64,1024]{1,0:T(8,128)(2,1)S(1)}, u32[]{:S(2)}, u32[]{:S(2)}) collective-permute-start(bf16[64,1024]{1,0:T(8,128)(2,1)S(1)} %add_convert_fusion.v_ref), channel_id=1, source_target_pairs={{0,3},{1,2},{2,1},{3,0},{4,7},{5,6},{6,5},{7,4},{8,11},{9,10},{10,... | collective-permute-start | bytes 393224 | tf_op jit(solution)/shard_map/ppermute | solution.py:366
  59.5 5.1 %collective-permute-start.7 = (bf16[64,1024]{1,0:T(8,128)(2,1)S(1)}, bf16[64,1024]{1,0:T(8,128)(2,1)S(1)}, u32[]{:S(2)}, u32[]{:S(2)}) collective-permute-start(bf16[64,1024]{1,0:T(8,128)(2,1)S(1)} %add_convert_fusion.v_ref), channel_id=1, source_target_pairs={{0,1},{1,0},{2,3},{3,2},{4,5},{5,4},{6,7},{7,6},{8,9},{9,8},{10,11... | collective-permute-start | bytes 393224 | tf_op jit(solution)/shard_map/ppermute | solution.py:366
